TPU v7x, 128 devices: a whole 4x4x4 slice. The times are simulated.
128 devices in a mesh: row: 8 (over x, core), col: 16 (over y, z).
Axes of the slice: x: 4, y: 4, z: 4, core: 2. Of those that a mesh axis runs over, the one named last changes fastest.
Arguments:
- blocks_a: bfloat16 [64, 256, 138, 138], P('row', 'col'), may hold values from -6 to 6
- pattern_a: int32 [64, 256], P('row', 'col'), may hold values 0 or 1
- blocks_b: bfloat16 [256, 16, 138, 138], P('col'), may hold values from -0.0625 to 0.0625
- filter_mask: int32 [64, 16], P('row', 'col'), may hold values 0 or 1
- task_brick: int32 [64, 16], P('row', 'col'), may hold values from 0 to 127
- basis_rows: bfloat16 [64, 138, 16384], P('row'), may hold values from -0.5 to 0.5
- basis_cols: bfloat16 [16, 138, 16384], P('col'), may hold values from -0.5 to 0.5
- kernel: float32 [1024, 2048], P(('row', 'col')), may hold values from 0.1 to 10
Outputs:
- density: bfloat16 [64, 16, 138, 138], P('row', 'col')
- potential: float32 [1024, 2048], P('row', 'col')
Inputs may be any that keep to these rules, and one draw needn't show every extreme that they name: `pattern_a`: 1 marks a block that is kept. `filter_mask`: 1 marks a product block that is kept.
All inputs are finite; a program needn't handle non-finite values.
Results may differ from a plain program's by a relative error of at most 0.0028.
Values may be sent and summed in bfloat16 or wider, within the bound.
No kernel may reach another device: no remote copies, remote signals or barrier semaphores. Data moves between devices by JAX's collectives and lax.ppermute only.
A program may use at most 576 MiB of HBM per device.

v0:
```python
import functools
import math

import jax
import jax.numpy as jnp
import numpy as np
from jax import lax
from jax.experimental import pallas as pl
from jax.experimental.pallas import tpu as pltpu
from jax.sharding import PartitionSpec as P

BS = 138
MIB = 1 << 20
HIGH = lax.Precision.HIGHEST
F32 = jnp.float32
BF16 = jnp.bfloat16
I16 = jnp.int16
WIDE = 2304
SPAN = 1152
ROWS = (560, 544)
CUT = (0, 560)
TOP = 288
FOLD = 80
POINTS = 2048


def widen(tail):
    return jnp.concatenate([tail.astype(F32), jnp.zeros(tail.shape[:-1] + (128 - tail.shape[-1],), F32)], axis=-1)


def place_tails(tails, out, rows):
    lane = lax.broadcasted_iota(jnp.int32, (16, 128), 1) // 16
    for half in range(2):
        rest = jnp.zeros((16, 128), F32)
        for n in range(8):
            tail = tails[half * 8 + n]
            rest = jnp.where(lane == n, pltpu.roll(tail, 16 * n, 1) if n else tail, rest)
        out(half, rest.astype(BF16))


def pack_left_kernel(pairs, mask, blocks, after, out):
    def step(p, carry):
        pair = jnp.transpose(blocks[:, pl.ds(2 * p, 2)], (1, 0, 2, 3)).reshape(16, 16, BS)
        wide = jnp.swapaxes(pair, 0, 1)
        rows = pl.ds(pl.multiple_of(16 * p, 16), 16)
        tails = []
        for k in range(16):
            at = SPAN * (k // 8) + 128 * (k % 8)
            out[rows, at : at + 128] = wide[k, :, :128] * mask[k]
            tails.append(widen(wide[k, :, 128:] * mask[k, :, : BS - 128]))

        def put(half, value):
            out[rows, SPAN * half + 1024 : SPAN * half + 1152] = value

        place_tails(tails, put, rows)
        return carry

    lax.fori_loop(0, pairs, step, 0)


def pack_left(half, mask, blocks, after):
    count = (14, 34)[half]
    return pl.pallas_call(
        functools.partial(pack_left_kernel, count // 2),
        grid=(ROWS[half] // 8 // count,),
        in_specs=[
            pl.BlockSpec((16, 16, 128), lambda g: (0, 0, 0)),
            pl.BlockSpec(
                (pl.Element(8), pl.Element(count), pl.Element(16), pl.Element(BS)),
                lambda g: (0, CUT[half] // 8 + count * g, 0, 0),
            ),
            pl.BlockSpec(memory_space=pl.ANY),
        ],
        out_specs=pl.BlockSpec((count * 8, WIDE), lambda g: (g, 0)),
        out_shape=jax.ShapeDtypeStruct((ROWS[half], WIDE), BF16),
        compiler_params=pltpu.CompilerParams(vmem_limit_bytes=32 * MIB),
        cost_estimate=pl.CostEstimate(flops=1 << 24, bytes_accessed=7 * MIB, transcendentals=0),
        name="pack_left",
    )(mask, blocks, after)


def pack_right_kernel(blocks, near):
    base = pl.program_id(0) % 4 * 2

    def step(n, carry):
        k = base + n
        for c in range(0, 144, 16):
            if c < 128:
                rows = pl.ds(pl.multiple_of(128 * k + c, 16), 16)
                square = blocks[n, c : c + 16]
            else:
                rows = pl.ds(pl.multiple_of(1024 + 16 * k, 16), 16)
                square = jnp.concatenate([blocks[n, 128:BS], jnp.zeros((144 - BS, 16, BS), BF16)], axis=0)
            near[:, rows, :] = jnp.swapaxes(square, 0, 1)
        return carry

    lax.fori_loop(0, 2, step, 0)


def pack_right(blocks):
    return pl.pallas_call(
        pack_right_kernel,
        grid=(8,),
        in_specs=[pl.BlockSpec((2, BS, 16, BS), lambda g: (g, 0, 0, 0))],
        out_specs=pl.BlockSpec((16, SPAN, BS), lambda g: (0, g // 4, 0)),
        out_shape=jax.ShapeDtypeStruct((16, WIDE, BS), BF16),
        compiler_params=pltpu.CompilerParams(vmem_limit_bytes=36 * MIB),
        cost_estimate=pl.CostEstimate(flops=1 << 24, bytes_accessed=38 * MIB, transcendentals=0),
        name="pack_right",
    )(blocks)


def lanes(rows):
    return lax.broadcasted_iota(jnp.int32, (rows, 128), 1)


def scale_of(most):
    power = jnp.floor(jnp.log2(jnp.maximum(jnp.full((1, 128), most, F32), 1e-30))) + 1.0
    return power, 32000.0 * jnp.exp2(-power)


def gain_of(coded):
    power = jnp.max(jnp.where(lanes(16) % 16 == 15, coded[0:16], -1000.0))
    return jnp.exp2(jnp.full((1, 128), power, F32)) * (1.0 / 32000.0)


def code(value, gain):
    return jnp.round(value * gain).astype(jnp.int32).astype(I16)


def code_tail(value, gain, power):
    coded = jnp.where(lanes(value.shape[0]) % 16 == 15, jnp.broadcast_to(power, value.shape), jnp.round(value * gain))
    return coded.astype(jnp.int32).astype(I16)


def plain(value):
    return value.astype(jnp.int32).astype(F32)


def product_kernel(half, d, spot, left, near, after, out, held):
    rows = ROWS[half]
    coded = d != 0
    group = (spot[half] + d) % 4
    slot = lanes(rows) // 16
    tail = jnp.zeros((rows, 128), F32)
    for n in range(4):
        both = jnp.dot(left[...], near[4 * group + n if half == 0 else 4 * n + group], preferred_element_type=F32)
        if coded:
            held[n] = both[:, :128]
        else:
            out[n * rows : (n + 1) * rows, :] = both[:, :128]
        piece = widen(both[:, 128:])
        tail = jnp.where(slot == n, pltpu.roll(piece, 16 * n, 1) if n else piece, tail)
    high, low = tail[:TOP], jnp.concatenate([tail[TOP:], jnp.zeros((2 * TOP - rows, 128), F32)], axis=0)
    folded = jnp.where(lanes(TOP) < 64, high, pltpu.roll(low, 64, 1))
    if coded:
        power, gain = scale_of(jnp.maximum(jnp.max(jnp.abs(held[...])), jnp.max(jnp.abs(folded))))
        for n in range(4):
            out[n * rows : (n + 1) * rows, :] = code(held[n], gain)
        out[4 * rows : 4 * rows + TOP, :] = code_tail(folded, gain, power)
    else:
        out[4 * rows : 4 * rows + TOP, :] = folded


def product_group(half, d, spot, left, near, after):
    rows = ROWS[half]
    coded = d != 0
    vmem = pl.BlockSpec(memory_space=pltpu.VMEM)
    return pl.pallas_call(
        functools.partial(product_kernel, half, d),
        in_specs=[pl.BlockSpec(memory_space=pltpu.SMEM), vmem, vmem, pl.BlockSpec(memory_space=pl.ANY)],
        out_specs=vmem,
        out_shape=jax.ShapeDtypeStruct((4 * rows + TOP, 128), I16 if coded else F32),
        scratch_shapes=[pltpu.VMEM((4, rows, 128), F32)],
        compiler_params=pltpu.CompilerParams(vmem_limit_bytes=12 * MIB),
        cost_estimate=pl.CostEstimate(flops=2 * 560 * WIDE * 1024, bytes_accessed=8 * MIB, transcendentals=0),
        name="product_coded" if coded else "product_own",
    )(spot, left, near, after)


def merge_kernel(half, place, own, in1, in2, in3, after, mine, out1, out2, out3, held):
    rows = ROWS[half]
    parts = (in1, in2, in3)
    tails = [plain(p[4 * rows : 4 * rows + TOP, :]) for p in parts]
    gains = [gain_of(t) for t in tails]
    for n in range(4):
        here = slice(n * rows, (n + 1) * rows)
        total = own[here, :]
        for p, g in zip(parts, gains):
            total = total + plain(p[here, :]) * g
        held[n] = total
    folded = own[4 * rows : 4 * rows + TOP, :]
    for t, g in zip(tails, gains):
        folded = folded + t * g
    last = jnp.concatenate([folded[3 * FOLD :], jnp.zeros((4 * FOLD - TOP, 128), F32)], axis=0)
    pieces = [folded[0:FOLD], folded[FOLD : 2 * FOLD], folded[2 * FOLD : 3 * FOLD], last]
    slot = lanes(FOLD) // 16 % 4
    for s in range(4):

        @pl.when(place[1 - half] == s)
        def _(s=s):
            for d, out in enumerate((mine, out1, out2, out3)):
                here = (s + d) % 4
                tail = jnp.zeros((FOLD, 128), F32)
                for q in range(4):
                    tail = jnp.where(slot == q, pltpu.roll(pieces[q], 16 * ((q - here) % 8), 1) if (q - here) % 8 else pieces[q], tail)
                main = held[here]
                if d == 0:
                    out[0:rows, :] = main
                    out[rows : rows + FOLD, :] = tail
                else:
                    tail = jnp.where(lanes(FOLD) % 16 < 10, tail, 0.0)
                    power, gain = scale_of(jnp.maximum(jnp.max(jnp.abs(main)), jnp.max(jnp.abs(tail))))
                    out[0:rows, :] = code(main, gain)
                    out[rows : rows + FOLD, :] = code_tail(tail, gain, power)


def merge(half, place, own, parts, after):
    vmem = pl.BlockSpec(memory_space=pltpu.VMEM)
    return pl.pallas_call(
        functools.partial(merge_kernel, half),
        in_specs=[pl.BlockSpec(memory_space=pltpu.SMEM)] + [vmem] * 4 + [pl.BlockSpec(memory_space=pl.ANY)],
        out_specs=[vmem] * 4,
        out_shape=[jax.ShapeDtypeStruct((ROWS[half] + FOLD, 128), t) for t in (F32, I16, I16, I16)],
        scratch_shapes=[pltpu.VMEM((4, ROWS[half], 128), F32)],
        compiler_params=pltpu.CompilerParams(vmem_limit_bytes=8 * MIB),
        cost_estimate=pl.CostEstimate(flops=1 << 22, bytes_accessed=4 * MIB, transcendentals=0),
        name="merge",
    )(place, own, *parts, after)


def turn(dy, dz):
    return [(4 * y + z, (y + dy) % 4 * 4 + (z + dz) % 4) for y in range(4) for z in range(4)]


def send(array, axis, d):
    return lax.ppermute(array, "col", turn(d, 0) if axis == 0 else turn(0, d))


def exchange_products(blocks_a, pattern, blocks_b):
    place = lax.axis_index("col").astype(jnp.int32)
    spot = jnp.stack([place // 4, place % 4])
    mask = jnp.broadcast_to(jnp.tile(pattern.T, (1, 2))[:, :, None], (16, 16, 128)).astype(BF16)
    blocks_a = jnp.transpose(blocks_a, (0, 2, 1, 3))
    near = pack_right(jnp.transpose(blocks_b, (0, 2, 1, 3)))
    after = near
    parts, owns = ([], []), []
    lefts = []
    for half in range(2):
        left = pack_left(half, mask, blocks_a, after)
        lefts.append(left)
        after = left
        for d in (2, 1, 3):
            after = product_group(half, d, spot, left, near, after)
            parts[half].append(send(after, half, d))
    for half in range(2):
        after = product_group(half, 0, spot, lefts[half], near, after)
        owns.append(after)

    def finish(half, after):
        mine, *outs = merge(half, spot, owns[half], parts[half], after)
        return mine, [send(outs[d - 1], 1 - half, d) for d in (2, 1, 3)]

    return finish, after


def collocate_kernel(half, keep, ids, own, in1, in2, in3, cols, rows, *rest):
    if half == 0:
        density, out, stacked, right = rest
        before = None
    else:
        before, density, out, stacked, right = rest
    count = ROWS[half]

    @pl.when(pl.program_id(0) == 0)
    def _():
        main, fold = own[0:count, :], own[count : count + FOLD, :]
        for part in (in1, in2, in3):
            extra = plain(part[count : count + FOLD, :])
            gain = gain_of(extra)
            main, fold = main + plain(part[0:count, :]) * gain, fold + extra * gain
        tails = []
        for base, total in ((0, TOP), (4, count - TOP)):
            for q in range(4):
                piece = fold[0 : min(FOLD, total - q * FOLD)]
                shift = (128 - 16 * (q + base)) % 128
                tails.append(pltpu.roll(piece, shift, 1) if shift else piece)
        tail = jnp.where(lanes(count) < BS - 128, jnp.concatenate(tails, axis=0), 0.0)
        kept = keep[...][None]
        main = (main.reshape(count // 8, 8, 128) * kept).reshape(count, 128).astype(BF16)
        tail = (tail.reshape(count // 8, 8, 128) * kept).reshape(count, 128).astype(BF16)
        stacked[:, 0:128] = main
        stacked[:, 128:256] = tail
        density[:, :, 0:128] = main.reshape(count // 8, 8, 128)
        density[:, :, 128:BS] = tail.reshape(count // 8, 8, 128)[:, :, : BS - 128]
        right[128:256, :] = jnp.zeros((128, POINTS), BF16)

    right[0:BS, :] = cols[0]
    for t in range(POINTS // 256):
        here = slice(t * 256, (t + 1) * 256)
        inner = jnp.dot(stacked[...], right[:, here], preferred_element_type=F32).reshape(count // 8, 8, 256)
        total = jnp.sum(inner * rows[:, :, here].astype(F32), axis=0)
        within = slice(t % 4 * 256, t % 4 * 256 + 256)
        if half == 1:
            total = total + before[t // 4, :, within]
        out[t // 4, :, within] = total
    if half == 1:
        for n in range(POINTS // 1024):
            out[n, :, 1024:1152] = ids[...]


def collocate(half, keep, ids, own, parts, basis_cols, basis_rows, before):
    count = ROWS[half]
    unit = pl.BlockSpec((count + FOLD, 128), lambda g: (0, 0))
    small = pl.BlockSpec((8, 128), lambda g: (0, 0))
    wide = 1152 if half else 1024
    many = count // 8
    return pl.pallas_call(
        functools.partial(collocate_kernel, half),
        grid=(16384 // POINTS,),
        in_specs=[small, small]
        + [unit] * 4
        + [
            pl.BlockSpec((1, BS, POINTS), lambda g: (0, 0, g)),
            pl.BlockSpec(
                (pl.Element(many), pl.Element(8), pl.Element(POINTS)), lambda g: (CUT[half] // 8, 0, g * POINTS)
            ),
        ]
        + [pl.BlockSpec((POINTS // 1024, 8, 1024), lambda g: (g, 0, 0))] * half,
        out_specs=[
            pl.BlockSpec((many, 8, BS), lambda g: (0, 0, 0)),
            pl.BlockSpec((POINTS // 1024, 8, wide), lambda g: (g, 0, 0)),
        ],
        scratch_shapes=[pltpu.VMEM((count, 256), BF16), pltpu.VMEM((256, POINTS), BF16)],
        out_shape=[
            jax.ShapeDtypeStruct((many, 8, BS), BF16),
            jax.ShapeDtypeStruct((16, 8, wide), F32),
        ],
        compiler_params=pltpu.CompilerParams(vmem_limit_bytes=16 * MIB),
        cost_estimate=pl.CostEstimate(
            flops=2 * count * 256 * 16384, bytes_accessed=(count + 144) * 16384 * 2, transcendentals=0
        ),
        name="collocate",
    )(keep, ids, own, *parts, basis_cols, basis_rows, *before)


def bricks_kernel(points, out):
    owners = jnp.sum(points[:, :, 1024:1152].reshape(128, 128), axis=0, keepdims=True).astype(jnp.int32)
    onehot = (owners == lax.broadcasted_iota(jnp.int32, (128, 128), 0)).astype(F32)
    held = points[:, :, 0:1024].reshape(128, 1024)
    out[...] = jnp.dot(onehot, held, precision=HIGH, preferred_element_type=F32)


def sum_bricks(points):
    return pl.pallas_call(
        bricks_kernel,
        out_shape=jax.ShapeDtypeStruct((128, 1024), F32),
        compiler_params=pltpu.CompilerParams(vmem_limit_bytes=8 * MIB),
        cost_estimate=pl.CostEstimate(flops=2 * 128 * 128 * 1024, bytes_accessed=MIB, transcendentals=0),
        name="sum_bricks",
    )(points)


def tables():
    a = np.arange(16)
    outer = 2.0 * math.pi * (np.outer(a, a) % 16) / 16
    eye = np.eye(8)
    ck, sk = np.kron(eye, np.cos(outer)), np.kron(eye, np.sin(outer))
    b = np.arange(128)
    inner = 2.0 * math.pi * (np.outer(b, b) % 128) / 128
    c, s = np.cos(inner), np.sin(inner)
    twist = 2.0 * math.pi * np.outer(np.tile(a, 8), b) / 2048
    first = np.concatenate([ck, -sk], 0)
    second = np.block([[c, -s], [s, c]])
    third = np.block([[c, s], [-s, c]])
    last = np.concatenate([ck, -sk], 1) / 2048
    return [np.asarray(t, np.float32) for t in (first, second, third, last, np.cos(twist), np.sin(twist))]


def filter_kernel(own, in1, in2, in3, kern, first, second, third, last, tc, ts, out):
    def dot(p, q):
        return jnp.dot(p, q, precision=HIGH, preferred_element_type=F32)

    grid = (own[...] + in1[...]) + (in2[...] + in3[...])
    grid = jnp.concatenate([grid[:, y * 128 : y * 128 + 128] for y in range(8)], axis=0)
    section = dot(first[...], grid)
    re, im = section[:128], section[128:]
    c, s = tc[...], ts[...]
    spec = dot(jnp.concatenate([re * c + im * s, im * c - re * s], axis=1), second[...])
    k = kern[...]
    back = dot(spec * jnp.concatenate([k, k], axis=1), third[...])
    re, im = back[:, :128], back[:, 128:]
    turned = jnp.concatenate([re * c - im * s, im * c + re * s], axis=0)
    result = dot(last[...], turned)
    for y in range(8):
        out[:, y, :] = result[y * 16 : y * 16 + 16]


def filter_rows(pieces, kern):
    return pl.pallas_call(
        filter_kernel,
        out_shape=jax.ShapeDtypeStruct((16, 8, 128), F32),
        compiler_params=pltpu.CompilerParams(vmem_limit_bytes=8 * MIB),
        cost_estimate=pl.CostEstimate(flops=1 << 26, bytes_accessed=MIB, transcendentals=0),
        name="filter_rows",
    )(*pieces, kern, *tables())


def scatter_rows(partial):
    place = lax.axis_index("row")
    x, core = place // 2, place % 2
    halves = partial.reshape(4, 2, 16, 1024)
    away = lax.dynamic_index_in_dim(halves, 1 - core, 1, keepdims=False)
    mine = lax.dynamic_index_in_dim(halves, core, 1, keepdims=False)
    mine = mine + lax.ppermute(away, "row", [(r, r ^ 1) for r in range(8)])
    pieces = [lax.dynamic_index_in_dim(mine, x, 0, keepdims=False)]
    for d in (1, 2, 3):
        part = lax.dynamic_index_in_dim(mine, (x + d) % 4, 0, keepdims=False)
        pieces.append(lax.ppermute(part, "row", [(r, (r + 2 * d) % 8) for r in range(8)]))
    return pieces


def shards(blocks_a, pattern_a, blocks_b, filter_mask, task_brick, basis_rows, basis_cols, kernel):
    kern = jnp.transpose(kernel.reshape(8, 128, 16), (0, 2, 1)).reshape(128, 128)
    lane = jnp.arange(128, dtype=jnp.int32)
    owners = jnp.where(lane // 8 == lax.axis_index("col"), jnp.tile(task_brick.reshape(8), 16), 0)
    ids = jnp.concatenate([owners.astype(F32)[None], jnp.zeros((7, 128), F32)], axis=0)
    keep = jnp.broadcast_to(filter_mask.reshape(8, 1).astype(F32), (8, 128))
    by_point = jnp.transpose(basis_rows, (1, 0, 2))
    finish, after = exchange_products(blocks_a, pattern_a, blocks_b)
    densities, before, sums = [], [], []
    for half in range(2):
        sums.append(finish(half, after))
        after = sums[-1][0]
    for half in range(2):
        own, parts = sums[half]
        density, points = collocate(half, keep, ids, own, parts, basis_cols, by_point, before)
        densities.append(density)
        before = [points]
    points = lax.all_to_all(points, "col", split_axis=0, concat_axis=0, tiled=True)
    pieces = scatter_rows(sum_bricks(points))
    filtered = filter_rows(pieces, kern)
    potential = lax.all_to_all(filtered, "col", split_axis=0, concat_axis=0, tiled=True)
    density = jnp.transpose(jnp.concatenate(densities, axis=0), (1, 0, 2))
    return density[:, None], potential.reshape(128, 128)


def solution(mesh):
    return jax.shard_map(
        shards,
        mesh=mesh,
        in_specs=(
            P("row", "col", None, None),
            P("row", "col"),
            P("col", None, None, None),
            P("row", "col"),
            P("row", "col"),
            P("row", None, None),
            P("col", None, None),
            P(("row", "col"), None),
        ),
        out_specs=(P("row", "col", None, None), P("row", "col")),
        check_vma=False,
    )
```

profile of v0, /device:TPU:0, one launch (start us, length us, event | category | flops | bytes accessed | tf_op | source)
XLA Modules:
  0.0 175.4 jit_solution(7548786343843653178)
XLA Ops:
  0.7 6.1 %copy-done.8 = bf16[16,16,138,138]{3,1,2,0:T(8,128)(2,1)S(1)} copy-done((bf16[16,16,138,138]{3,1,2,0:T(8,128)(2,1)S(1)}, bf16[16,16,138,138]{3,1,2,0:T(8,128)(2,1)}, u32[]{:S(2)}) %copy-start.8) | copy-done | bytes 9750552
  6.8 11.3 %pack_right.1.after.near = bf16[16,2304,138]{2,1,0:T(8,128)(2,1)} custom-call(bf16[16,138,16,138]{3,2,1,0:T(8,128)(2,1)S(1)} %bitcast.36), custom_call_target="tpu_custom_call" | custom-call | flops 16777216 | bytes 39845888 | tf_op jit(solution)/shard_map/pack_right/pallas_call | solution.py:101
  18.4 3.6 %copy-done.6 = bf16[8,16,138,138]{3,1,2,0:T(8,128)(2,1)S(1)} copy-done((bf16[8,16,138,138]{3,1,2,0:T(8,128)(2,1)S(1)}, bf16[8,16,138,138]{3,1,2,0:T(8,128)(2,1)}, u32[]{:S(2)}) %copy-start.6) | copy-done | bytes 4875288
  21.9 4.8 %pack_left.2.left.after = bf16[560,2304]{1,0:T(8,128)(2,1)S(1)} custom-call(bf16[16,16,128]{2,1,0:T(8,128)(2,1)S(1)} %broadcast_in_dim.21.mask, bf16[8,138,16,138]{3,2,1,0:T(8,128)(2,1)S(1)} %bitcast.32, bf16[16,2304,138]{2,1,0:T(8,128)(2,1)} %pack_right.1.after.near), custom_call_target="tpu_custom_call" | custom-call | flops 16777216 | bytes 7340032 | tf_op jit(solution)/shard_map/pack_left/pallas_call | solution.py:63
  28.3 3.9 %product_coded.6.after = s16[2528,128]{1,0:T(8,128)(2,1)S(1)} custom-call(s32[2]{0:T(128)S(1)} %pad_add_fusion.spot.place, bf16[560,2304]{1,0:T(8,128)(2,1)S(1)} %pack_left.2.left.after, bf16[16,2304,138]{2,1,0:T(8,128)(2,1)S(1)} %copy-done, bf16[560,2304]{1,0:T(8,128)(2,1)S(1)} %pack_left.2.left.after), custom_call_target="tpu_custom_call" | custom-call | flops 2642411520 | bytes 8388608 | tf_op jit(solution)/shard_map/product_coded/pallas_call | solution.py:169
  32.2 3.4 %collective-permute-start = (s16[2528,128]{1,0:T(8,128)(2,1)S(1)}, s16[2528,128]{1,0:T(8,128)(2,1)}, u32[]{:S(2)}, u32[]{:S(2)}) collective-permute-start(s16[2528,128]{1,0:T(8,128)(2,1)S(1)} %product_coded.6.after), channel_id=1, source_target_pairs={{0,8},{1,9},{2,10},{3,11},{4,12},{5,13},{6,14},{7,15},{8,0},{9,1},... | collective-permute-start | bytes 1941512 | tf_op jit(solution)/shard_map/ppermute | solution.py:237
  35.5 3.9 %product_coded.7.after = s16[2528,128]{1,0:T(8,128)(2,1)S(1)} custom-call(s32[2]{0:T(128)S(1)} %pad_add_fusion.spot.place, bf16[560,2304]{1,0:T(8,128)(2,1)S(1)} %pack_left.2.left.after, bf16[16,2304,138]{2,1,0:T(8,128)(2,1)S(1)} %copy-done, s16[2528,128]{1,0:T(8,128)(2,1)S(1)} %product_coded.6.after), custom_call_target="tpu_custom_call" | custom-call | flops 2642411520 | bytes 8388608 | tf_op jit(solution)/shard_map/product_coded/pallas_call | solution.py:169
  40.1 3.9 %product_coded.8.after = s16[2528,128]{1,0:T(8,128)(2,1)S(1)} custom-call(s32[2]{0:T(128)S(1)} %pad_add_fusion.spot.place, bf16[560,2304]{1,0:T(8,128)(2,1)S(1)} %pack_left.2.left.after, bf16[16,2304,138]{2,1,0:T(8,128)(2,1)S(1)} %copy-done, s16[2528,128]{1,0:T(8,128)(2,1)S(1)} %product_coded.7.after), custom_call_target="tpu_custom_call" | custom-call | flops 2642411520 | bytes 8388608 | tf_op jit(solution)/shard_map/product_coded/pallas_call | solution.py:169
  46.8 3.6 %copy-done.7 = bf16[8,16,138,138]{3,1,2,0:T(8,128)(2,1)S(1)} copy-done((bf16[8,16,138,138]{3,1,2,0:T(8,128)(2,1)S(1)}, bf16[8,16,138,138]{3,1,2,0:T(8,128)(2,1)}, u32[]{:S(2)}) %copy-start.7) | copy-done | bytes 4875288
  50.4 4.7 %pack_left.3.left.after = bf16[544,2304]{1,0:T(8,128)(2,1)S(1)} custom-call(bf16[16,16,128]{2,1,0:T(8,128)(2,1)S(1)} %broadcast_in_dim.21.mask, bf16[8,138,16,138]{3,2,1,0:T(8,128)(2,1)S(1)} %bitcast.33, s16[2528,128]{1,0:T(8,128)(2,1)S(1)} %product_coded.8.after), custom_call_target="tpu_custom_call" | custom-call | flops 16777216 | bytes 7340032 | tf_op jit(solution)/shard_map/pack_left/pallas_call | solution.py:63
  55.1 3.8 %product_coded.9.after = s16[2464,128]{1,0:T(8,128)(2,1)S(1)} custom-call(s32[2]{0:T(128)S(1)} %pad_add_fusion.spot.place, bf16[544,2304]{1,0:T(8,128)(2,1)S(1)} %pack_left.3.left.after, bf16[16,2304,138]{2,1,0:T(8,128)(2,1)S(1)} %copy-done, bf16[544,2304]{1,0:T(8,128)(2,1)S(1)} %pack_left.3.left.after), custom_call_target="tpu_custom_call" | custom-call | flops 2642411520 | bytes 8388608 | tf_op jit(solution)/shard_map/product_coded/pallas_call | solution.py:169
  58.9 4.6 %product_coded.10.after = s16[2464,128]{1,0:T(8,128)(2,1)} custom-call(s32[2]{0:T(128)S(1)} %pad_add_fusion.spot.place, bf16[544,2304]{1,0:T(8,128)(2,1)S(1)} %pack_left.3.left.after, bf16[16,2304,138]{2,1,0:T(8,128)(2,1)S(1)} %copy-done, s16[2464,128]{1,0:T(8,128)(2,1)S(1)} %product_coded.9.after), custom_call_target="tpu_custom_call" | custom-call | flops 2642411520 | bytes 8388608 | tf_op jit(solution)/shard_map/product_coded/pallas_call | solution.py:169
  65.4 4.6 %product_coded.11.after = s16[2464,128]{1,0:T(8,128)(2,1)} custom-call(s32[2]{0:T(128)S(1)} %pad_add_fusion.spot.place, bf16[544,2304]{1,0:T(8,128)(2,1)S(1)} %pack_left.3.left.after, bf16[16,2304,138]{2,1,0:T(8,128)(2,1)S(1)} %copy-done, s16[2464,128]{1,0:T(8,128)(2,1)} %product_coded.10.after), custom_call_target="tpu_custom_call" | custom-call | flops 2642411520 | bytes 8388608 | tf_op jit(solution)/shard_map/product_coded/pallas_call | solution.py:169
  74.2 6.4 %copy-done.1 = bf16[16,2304,138]{2,1,0:T(8,128)(2,1)S(1)} copy-done((bf16[16,2304,138]{2,1,0:T(8,128)(2,1)S(1)}, bf16[16,2304,138]{2,1,0:T(8,128)(2,1)}, u32[]{:S(2)}) %copy-start.1) | copy-done | bytes 10174488
  82.3 3.5 %product_own.2.after.own = f32[2528,128]{1,0:T(8,128)S(1)} custom-call(s32[2]{0:T(128)S(1)} %pad_add_fusion.spot.place, bf16[560,2304]{1,0:T(8,128)(2,1)S(1)} %copy-done.3, bf16[16,2304,138]{2,1,0:T(8,128)(2,1)S(1)} %copy-done.1, s16[2464,128]{1,0:T(8,128)(2,1)} %product_coded.11.after), custom_call_target="tpu_custom_call" | custom-call | flops 2642411520 | bytes 8388608 | tf_op jit(solution)/shard_map/product_own/pallas_call | solution.py:169
  85.9 3.4 %product_own.3.after.own = f32[2464,128]{1,0:T(8,128)S(1)} custom-call(s32[2]{0:T(128)S(1)} %pad_add_fusion.spot.place, bf16[544,2304]{1,0:T(8,128)(2,1)S(1)} %copy-done.5, bf16[16,2304,138]{2,1,0:T(8,128)(2,1)S(1)} %copy-done.1, f32[2528,128]{1,0:T(8,128)S(1)} %product_own.2.after.own), custom_call_target="tpu_custom_call" | custom-call | flops 2642411520 | bytes 8388608 | tf_op jit(solution)/shard_map/product_own/pallas_call | solution.py:169
  94.1 7.3 %collective-permute-done.8.in3 = s16[2464,128]{1,0:T(8,128)(2,1)S(1)} collective-permute-done((s16[2464,128]{1,0:T(8,128)(2,1)}, s16[2464,128]{1,0:T(8,128)(2,1)S(1)}, u32[]{:S(2)}, u32[]{:S(2)}) %collective-permute-start.8) | collective-permute-done | bytes 630816 | tf_op jit(solution)/shard_map/ppermute | solution.py:237
  101.4 4.1 %collective-permute-start.5 = (s16[640,128]{1,0:T(8,128)(2,1)S(1)}, s16[640,128]{1,0:T(8,128)(2,1)S(1)}, u32[]{:S(2)}, u32[]{:S(2)}) collective-permute-start(s16[640,128]{1,0:T(8,128)(2,1)S(1)} %get-tuple-element.17), channel_id=1, source_target_pairs={{0,3},{1,0},{2,1},{3,2},{4,7},{5,4},{6,5},{7,6},{8,11},{9,8},{10,9... | collective-permute-start | bytes 491528 | tf_op jit(solution)/shard_map/ppermute | solution.py:237
  111.3 11.7 %collocate.2 = (bf16[70,8,138]{2,1,0:T(8,128)(2,1)S(1)}, f32[16,8,1024]{2,1,0:T(8,128)S(1)}) custom-call(f32[8,128]{1,0:T(8,128)S(1)} %broadcast_in_dim.20.keep, f32[8,128]{1,0:T(8,128)S(1)} %concatenate.6.ids, f32[640,128]{1,0:T(8,128)S(1)} %get-tuple-element.14.own.after, s16[640,128]{1,0:T(8,128)(2,1)S(1)} %collective-permute-done.3.in1, ...), custom_call_target="tpu_custom_call" | custom-call | flops 4697620480 | bytes 23068672 | tf_op jit(solution)/shard_map/collocate/pallas_call | solution.py:318
  123.0 12.2 %collocate.3 = (bf16[68,8,138]{2,1,0:T(8,128)(2,1)S(1)}, f32[16,8,1152]{2,1,0:T(8,128)}) custom-call(f32[8,128]{1,0:T(8,128)S(1)} %broadcast_in_dim.20.keep, f32[8,128]{1,0:T(8,128)S(1)} %concatenate.6.ids, f32[624,128]{1,0:T(8,128)S(1)} %get-tuple-element.19.own, s16[624,128]{1,0:T(8,128)(2,1)S(1)} %collective-permute-done.9.in1, ...), custom_call_target="tpu_custom_call" | custom-call | flops 4563402752 | bytes 22544384 | tf_op jit(solution)/shard_map/collocate/pallas_call | solution.py:318
  135.2 5.0 %all-to-all-start = ((f32[16,8,1152]{2,1,0:T(8,128)}), f32[16,8,1152]{2,1,0:T(8,128)S(1)}, u32[]{:S(2)}, u32[]{:S(2)}) async-start(f32[16,8,1152]{2,1,0:T(8,128)} %get-tuple-element.25), calls=%async_computation | async-start | bytes 1179648 | tf_op jit(solution)/shard_map/all_to_all | solution.py:440
  140.3 10.4 %all-to-all-done.points = f32[16,8,1152]{2,1,0:T(8,128)S(1)} async-done(((f32[16,8,1152]{2,1,0:T(8,128)}), f32[16,8,1152]{2,1,0:T(8,128)S(1)}, u32[]{:S(2)}, u32[]{:S(2)}) %all-to-all-start) | async-done | bytes 589856 | tf_op jit(solution)/shard_map/all_to_all | solution.py:440
  163.6 3.5 %all-to-all-start.1 = ((f32[16,8,128]{2,1,0:T(8,128)}), f32[16,8,128]{2,1,0:T(8,128)S(1)}, u32[]{:S(2)}, u32[]{:S(2)}) async-start(f32[16,8,128]{2,1,0:T(8,128)} %filter_rows.1), calls=%async_computation.1 | async-start | bytes 131072 | tf_op jit(solution)/shard_map/all_to_all | solution.py:443
  168.0 6.7 %all-to-all-done.1 = f32[16,8,128]{2,1,0:T(8,128)S(1)} async-done(((f32[16,8,128]{2,1,0:T(8,128)}), f32[16,8,128]{2,1,0:T(8,128)S(1)}, u32[]{:S(2)}, u32[]{:S(2)}) %all-to-all-start.1) | async-done | bytes 65568 | tf_op jit(solution)/shard_map/all_to_all | solution.py:443
  (92 shorter events, 38.0 us)
Async XLA Ops:
  32.2 57.1 %collective-permute-start = (s16[2528,128]{1,0:T(8,128)(2,1)S(1)}, s16[2528,128]{1,0:T(8,128)(2,1)}, u32[]{:S(2)}, u32[]{:S(2)}) collective-permute-start(s16[2528,128]{1,0:T(8,128)(2,1)S(1)} %product_coded.6.after), channel_id=1, source_target_pairs={{0,8},{1,9},{2,10},{3,11},{4,12},{5,13},{6,14},{7,15},{8,0},{9,1},... | collective-permute-start | bytes 1941512 | tf_op jit(solution)/shard_map/ppermute | solution.py:237
  39.4 49.9 %collective-permute-start.1 = (s16[2528,128]{1,0:T(8,128)(2,1)S(1)}, s16[2528,128]{1,0:T(8,128)(2,1)}, u32[]{:S(2)}, u32[]{:S(2)}) collective-permute-start(s16[2528,128]{1,0:T(8,128)(2,1)S(1)} %product_coded.7.after), channel_id=1, source_target_pairs={{0,4},{1,5},{2,6},{3,7},{4,8},{5,9},{6,10},{7,11},{8,12},{9,13},{1... | collective-permute-start | bytes 1941512 | tf_op jit(solution)/shard_map/ppermute | solution.py:237
  44.0 28.2 %collective-permute-start.2 = (s16[2528,128]{1,0:T(8,128)(2,1)S(1)}, s16[2528,128]{1,0:T(8,128)(2,1)}, u32[]{:S(2)}, u32[]{:S(2)}) collective-permute-start(s16[2528,128]{1,0:T(8,128)(2,1)S(1)} %product_coded.8.after), channel_id=1, source_target_pairs={{0,12},{1,13},{2,14},{3,15},{4,0},{5,1},{6,2},{7,3},{8,4},{9,5},{1... | collective-permute-start | bytes 1941512 | tf_op jit(solution)/shard_map/ppermute | solution.py:237
  63.5 42.0 %collective-permute-start.7 = (s16[2464,128]{1,0:T(8,128)(2,1)}, s16[2464,128]{1,0:T(8,128)(2,1)}, u32[]{:S(2)}, u32[]{:S(2)}) collective-permute-start(s16[2464,128]{1,0:T(8,128)(2,1)} %product_coded.10.after), channel_id=1, source_target_pairs={{0,1},{1,2},{2,3},{3,0},{4,5},{5,6},{6,7},{7,4},{8,9},{9,10},{10,1... | collective-permute-start | bytes 1892360 | tf_op jit(solution)/shard_map/ppermute | solution.py:237
  70.0 31.4 %collective-permute-start.8 = (s16[2464,128]{1,0:T(8,128)(2,1)}, s16[2464,128]{1,0:T(8,128)(2,1)S(1)}, u32[]{:S(2)}, u32[]{:S(2)}) collective-permute-start(s16[2464,128]{1,0:T(8,128)(2,1)} %product_coded.11.after), channel_id=1, source_target_pairs={{0,3},{1,0},{2,1},{3,2},{4,7},{5,4},{6,5},{7,6},{8,11},{9,8},{10,9... | collective-permute-start | bytes 1892360 | tf_op jit(solution)/shard_map/ppermute | solution.py:237
  72.3 33.2 %collective-permute-start.6 = (s16[2464,128]{1,0:T(8,128)(2,1)}, s16[2464,128]{1,0:T(8,128)(2,1)S(1)}, u32[]{:S(2)}, u32[]{:S(2)}) collective-permute-start(s16[2464,128]{1,0:T(8,128)(2,1)} %copy-done.9), channel_id=1, source_target_pairs={{0,2},{1,3},{2,0},{3,1},{4,6},{5,7},{6,4},{7,5},{8,10},{9,11},{10,... | collective-permute-start | bytes 1892360 | tf_op jit(solution)/shard_map/ppermute | solution.py:237
  82.3 29.0 %slice-start = ((s8[4718592]{0:T(1024)(128)(4,1)}), s8[4194304]{0:T(1024)(128)(4,1)S(1)}, s32[]{:S(2)}) async-start(s8[4718592]{0:T(1024)(128)(4,1)} %bitcast.34), calls=%async_computation.2 | async-start | bytes 8388608
  92.4 18.8 %collective-permute-start.3 = (s16[640,128]{1,0:T(8,128)(2,1)S(1)}, s16[640,128]{1,0:T(8,128)(2,1)S(1)}, u32[]{:S(2)}, u32[]{:S(2)}) collective-permute-start(s16[640,128]{1,0:T(8,128)(2,1)S(1)} %get-tuple-element.15), channel_id=1, source_target_pairs={{0,2},{1,3},{2,0},{3,1},{4,6},{5,7},{6,4},{7,5},{8,10},{9,11},{10,... | collective-permute-start | bytes 491528 | tf_op jit(solution)/shard_map/ppermute | solution.py:237
  94.1 17.1 %collective-permute-start.4 = (s16[640,128]{1,0:T(8,128)(2,1)S(1)}, s16[640,128]{1,0:T(8,128)(2,1)S(1)}, u32[]{:S(2)}, u32[]{:S(2)}) collective-permute-start(s16[640,128]{1,0:T(8,128)(2,1)S(1)} %get-tuple-element.16), channel_id=1, source_target_pairs={{0,1},{1,2},{2,3},{3,0},{4,5},{5,6},{6,7},{7,4},{8,9},{9,10},{10,1... | collective-permute-start | bytes 491528 | tf_op jit(solution)/shard_map/ppermute | solution.py:237
  101.4 9.8 %collective-permute-start.5 = (s16[640,128]{1,0:T(8,128)(2,1)S(1)}, s16[640,128]{1,0:T(8,128)(2,1)S(1)}, u32[]{:S(2)}, u32[]{:S(2)}) collective-permute-start(s16[640,128]{1,0:T(8,128)(2,1)S(1)} %get-tuple-element.17), channel_id=1, source_target_pairs={{0,3},{1,0},{2,1},{3,2},{4,7},{5,4},{6,5},{7,6},{8,11},{9,8},{10,9... | collective-permute-start | bytes 491528 | tf_op jit(solution)/shard_map/ppermute | solution.py:237
  107.9 15.1 %collective-permute-start.10 = (s16[624,128]{1,0:T(8,128)(2,1)S(1)}, s16[624,128]{1,0:T(8,128)(2,1)S(1)}, u32[]{:S(2)}, u32[]{:S(2)}) collective-permute-start(s16[624,128]{1,0:T(8,128)(2,1)S(1)} %get-tuple-element.21), channel_id=1, source_target_pairs={{0,4},{1,5},{2,6},{3,7},{4,8},{5,9},{6,10},{7,11},{8,12},{9,13},{1... | collective-permute-start | bytes 479240 | tf_op jit(solution)/shard_map/ppermute | solution.py:237
  108.0 15.0 %collective-permute-start.11 = (s16[624,128]{1,0:T(8,128)(2,1)S(1)}, s16[624,128]{1,0:T(8,128)(2,1)S(1)}, u32[]{:S(2)}, u32[]{:S(2)}) collective-permute-start(s16[624,128]{1,0:T(8,128)(2,1)S(1)} %get-tuple-element.22), channel_id=1, source_target_pairs={{0,12},{1,13},{2,14},{3,15},{4,0},{5,1},{6,2},{7,3},{8,4},{9,5},{1... | collective-permute-start | bytes 479240 | tf_op jit(solution)/shard_map/ppermute | solution.py:237
  111.2 11.8 %collective-permute-start.9 = (s16[624,128]{1,0:T(8,128)(2,1)S(1)}, s16[624,128]{1,0:T(8,128)(2,1)S(1)}, u32[]{:S(2)}, u32[]{:S(2)}) collective-permute-start(s16[624,128]{1,0:T(8,128)(2,1)S(1)} %get-tuple-element.20), channel_id=1, source_target_pairs={{0,8},{1,9},{2,10},{3,11},{4,12},{5,13},{6,14},{7,15},{8,0},{9,1},... | collective-permute-start | bytes 479240 | tf_op jit(solution)/shard_map/ppermute | solution.py:237
  123.0 35.8 %copy-start.16 = (f32[8,2048]{1,0:T(8,128)S(1)}, f32[8,2048]{1,0:T(8,128)}, u32[]{:S(2)}) copy-start(f32[8,2048]{1,0:T(8,128)} %param.21) | copy-start | bytes 196612
  135.2 26.4 %copy-start.12 = (f32[256,128]{1,0:T(8,128)S(1)}, f32[256,128]{1,0:T(8,128)}, u32[]{:S(2)}) copy-start(f32[256,128]{1,0:T(8,128)} %constant.111.clone.first) | copy-start | bytes 393220
  135.2 26.4 %copy-start.13 = (f32[128,256]{1,0:T(8,128)S(1)}, f32[128,256]{1,0:T(8,128)}, u32[]{:S(2)}) copy-start(f32[128,256]{1,0:T(8,128)} %constant.114.clone.last) | copy-start | bytes 393220
  135.2 26.4 %copy-start.14 = (f32[128,128]{1,0:T(8,128)S(1)}, f32[128,128]{1,0:T(8,128)}, u32[]{:S(2)}) copy-start(f32[128,128]{1,0:T(8,128)} %constant.115.clone.tc) | copy-start | bytes 196612
  135.2 26.4 %copy-start.15 = (f32[128,128]{1,0:T(8,128)S(1)}, f32[128,128]{1,0:T(8,128)}, u32[]{:S(2)}) copy-start(f32[128,128]{1,0:T(8,128)} %constant.116.clone.ts) | copy-start | bytes 196612
  135.2 15.5 %all-to-all-start = ((f32[16,8,1152]{2,1,0:T(8,128)}), f32[16,8,1152]{2,1,0:T(8,128)S(1)}, u32[]{:S(2)}, u32[]{:S(2)}) async-start(f32[16,8,1152]{2,1,0:T(8,128)} %get-tuple-element.25), calls=%async_computation | async-start | bytes 1179648 | tf_op jit(solution)/shard_map/all_to_all | solution.py:440
  151.4 1.6 collective-permute-start.12
  153.1 6.1 %collective-permute-start.13 = (f32[16,1024]{1,0:T(8,128)S(1)}, f32[16,1024]{1,0:T(8,128)S(1)}, u32[]{:S(2)}, u32[]{:S(2)}) collective-permute-start(f32[16,1024]{1,0:T(8,128)S(1)} %get-tuple-element.28), channel_id=1, source_target_pairs={{0,32},{16,48},{32,64},{48,80},{64,96},{80,112},{96,0},{112,16},{1... | collective-permute-start | bytes 196616 | tf_op jit(solution)/shard_map/ppermute | solution.py:419
  154.6 6.3 %collective-permute-start.14 = (f32[16,1024]{1,0:T(8,128)S(1)}, f32[16,1024]{1,0:T(8,128)S(1)}, u32[]{:S(2)}, u32[]{:S(2)}) collective-permute-start(f32[16,1024]{1,0:T(8,128)S(1)} %get-tuple-element.27), channel_id=1, source_target_pairs={{0,64},{16,80},{32,96},{48,112},{64,0},{80,16},{96,32},{112,48},{1... | collective-permute-start | bytes 196616 | tf_op jit(solution)/shard_map/ppermute | solution.py:419
  157.4 4.3 %collective-permute-start.15 = (f32[16,1024]{1,0:T(8,128)S(1)}, f32[16,1024]{1,0:T(8,128)S(1)}, u32[]{:S(2)}, u32[]{:S(2)}) collective-permute-start(f32[16,1024]{1,0:T(8,128)S(1)} %get-tuple-element.26), channel_id=1, source_target_pairs={{0,96},{16,112},{32,0},{48,16},{64,32},{80,48},{96,64},{112,80},{1... | collective-permute-start | bytes 196616 | tf_op jit(solution)/shard_map/ppermute | solution.py:419
  163.6 11.1 %all-to-all-start.1 = ((f32[16,8,128]{2,1,0:T(8,128)}), f32[16,8,128]{2,1,0:T(8,128)S(1)}, u32[]{:S(2)}, u32[]{:S(2)}) async-start(f32[16,8,128]{2,1,0:T(8,128)} %filter_rows.1), calls=%async_computation.1 | async-start | bytes 131072 | tf_op jit(solution)/shard_map/all_to_all | solution.py:443
  (16 other events, 182.5 us)
where the time goes:
time: 176 us; the launch traced here: 175 us
  Pallas kernels  84.1 us (48%)
  starting transfers between devices  36.4 us (21%)
  waiting for transfers between devices  28.3 us (16%)
  local copies, waits for them, and re-layouts  24.4 us (14%)
    pallas_call x8, Pallas kernels, product_group(): pl.pallas_call(functools.partial(product_kernel, half, d), in_specs=[pl.B...  31.5 us
    pallas_call x2, Pallas kernels, collocate(): pl.pallas_call(functools.partial(collocate_kernel, half), grid=(16384 //...  23.9 us
    unnamed x45, local copies, waits for them, and re-layouts  23.6 us
    ppermute x12, starting transfers between devices, send(): return lax.ppermute(array, 'col', turn(d, 0) if axis == 0 else turn(0, d))  22 us
    pallas_call x1, Pallas kernels, pack_right(): pl.pallas_call(pack_right_kernel, grid=(8,), in_specs=[pl.BlockSpec((2, B...  11.3 us
    all_to_all x1, waiting for transfers between devices, shards(): lax.all_to_all(points, 'col', split_axis=0, concat_axis=0, tiled=True)  10.4 us
    pallas_call x2, Pallas kernels, pack_left(): pl.pallas_call(functools.partial(pack_left_kernel, count // 2), grid=(ROW...  9.5 us
    ppermute x12, waiting for transfers between devices, send(): return lax.ppermute(array, 'col', turn(d, 0) if axis == 0 else turn(0, d))  7.3 us
  transfers between devices with their start and end apart: 18, of which 6 were waited for; matrix products, arithmetic and copies ran while one was open for 1% of the time, Pallas kernels for 28%

commit v1 on v0

--- a/solution.py
+++ b/solution.py
@@ -24,6 +24,10 @@
 POINTS = 2048
 
 
+def in_hbm(array):
+    return pltpu.with_memory_space_constraint(array, pltpu.HBM)
+
+
 def widen(tail):
     return jnp.concatenate([tail.astype(F32), jnp.zeros(tail.shape[:-1] + (128 - tail.shape[-1],), F32)], axis=-1)
 
@@ -72,14 +76,14 @@
             pl.BlockSpec(memory_space=pl.ANY),
         ],
         out_specs=pl.BlockSpec((count * 8, WIDE), lambda g: (g, 0)),
-        out_shape=jax.ShapeDtypeStruct((ROWS[half], WIDE), BF16),
+        out_shape=pltpu.VMEM((ROWS[half], WIDE), BF16),
         compiler_params=pltpu.CompilerParams(vmem_limit_bytes=32 * MIB),
         cost_estimate=pl.CostEstimate(flops=1 << 24, bytes_accessed=7 * MIB, transcendentals=0),
         name="pack_left",
-    )(mask, blocks, after)
-
-
-def pack_right_kernel(blocks, near):
+    )(mask, in_hbm(blocks), after)
+
+
+def pack_right_kernel(blocks, near, rest):
     base = pl.program_id(0) % 4 * 2
 
     def step(n, carry):
@@ -91,7 +95,13 @@
             else:
                 rows = pl.ds(pl.multiple_of(1024 + 16 * k, 16), 16)
                 square = jnp.concatenate([blocks[n, 128:BS], jnp.zeros((144 - BS, 16, BS), BF16)], axis=0)
-            near[:, rows, :] = jnp.swapaxes(square, 0, 1)
+            turned = jnp.swapaxes(square, 0, 1)
+            near[:, rows, :] = turned[:, :, :128]
+
+            def put(half, value, rows=rows):
+                rest[rows, 128 * half : 128 * half + 128] = value
+
+            place_tails([widen(turned[j, :, 128:]) for j in range(16)], put, rows)
         return carry
 
     lax.fori_loop(0, 2, step, 0)
@@ -102,12 +112,41 @@
         pack_right_kernel,
         grid=(8,),
         in_specs=[pl.BlockSpec((2, BS, 16, BS), lambda g: (g, 0, 0, 0))],
-        out_specs=pl.BlockSpec((16, SPAN, BS), lambda g: (0, g // 4, 0)),
-        out_shape=jax.ShapeDtypeStruct((16, WIDE, BS), BF16),
-        compiler_params=pltpu.CompilerParams(vmem_limit_bytes=36 * MIB),
-        cost_estimate=pl.CostEstimate(flops=1 << 24, bytes_accessed=38 * MIB, transcendentals=0),
+        out_specs=[
+            pl.BlockSpec((16, SPAN, 128), lambda g: (0, g // 4, 0)),
+            pl.BlockSpec((SPAN, 256), lambda g: (g // 4, 0)),
+        ],
+        out_shape=[
+            pltpu.VMEM((16, WIDE, 128), BF16),
+            pltpu.VMEM((WIDE, 256), BF16),
+        ],
+        compiler_params=pltpu.CompilerParams(vmem_limit_bytes=24 * MIB),
+        cost_estimate=pl.CostEstimate(flops=1 << 24, bytes_accessed=30 * MIB, transcendentals=0),
         name="pack_right",
-    )(blocks)
+    )(in_hbm(blocks))
+
+
+def tails_kernel(half, left, rest, swap, after, out):
+    right = rest[...]
+    if half == 1:
+        right = jnp.dot(right, swap[...], preferred_element_type=F32).astype(BF16)
+    out[...] = jnp.dot(left[...], right, preferred_element_type=F32)
+
+
+def product_tails(half, left, rest, after):
+    lane = np.arange(256)
+    swap = np.zeros((256, 256), np.float32)
+    swap[lane, lane // 16 % 4 * 64 + lane // 64 * 16 + lane % 16] = 1.0
+    vmem = pl.BlockSpec(memory_space=pltpu.VMEM)
+    return pl.pallas_call(
+        functools.partial(tails_kernel, half),
+        in_specs=[vmem] * 3 + [pl.BlockSpec(memory_space=pl.ANY)],
+        out_specs=vmem,
+        out_shape=jax.ShapeDtypeStruct((ROWS[half], 256), F32),
+        compiler_params=pltpu.CompilerParams(vmem_limit_bytes=12 * MIB),
+        cost_estimate=pl.CostEstimate(flops=2 * 560 * WIDE * 256, bytes_accessed=4 * MIB, transcendentals=0),
+        name="product_tails",
+    )(left, rest, jnp.asarray(swap, BF16), after)
 
 
 def lanes(rows):
@@ -137,22 +176,31 @@
     return value.astype(jnp.int32).astype(F32)
 
 
-def product_kernel(half, d, spot, left, near, after, out, held):
+def product_kernel(half, d, spot, left, near, tails, after, out, held):
     rows = ROWS[half]
     coded = d != 0
     group = (spot[half] + d) % 4
-    slot = lanes(rows) // 16
-    tail = jnp.zeros((rows, 128), F32)
-    for n in range(4):
-        both = jnp.dot(left[...], near[4 * group + n if half == 0 else 4 * n + group], preferred_element_type=F32)
+    which = [4 * group + n if half == 0 else 4 * n + group for n in range(4)]
+    for pair in range(2):
+        both = jnp.dot(
+            left[...],
+            jnp.concatenate([near[which[2 * pair]], near[which[2 * pair + 1]]], axis=1),
+            preferred_element_type=F32,
+        )
         if coded:
-            held[n] = both[:, :128]
+            held[2 * pair] = both[:, :128]
+            held[2 * pair + 1] = both[:, 128:]
         else:
-            out[n * rows : (n + 1) * rows, :] = both[:, :128]
-        piece = widen(both[:, 128:])
-        tail = jnp.where(slot == n, pltpu.roll(piece, 16 * n, 1) if n else piece, tail)
+            out[2 * pair * rows : (2 * pair + 1) * rows, :] = both[:, :128]
+            out[(2 * pair + 1) * rows : (2 * pair + 2) * rows, :] = both[:, 128:]
+    tail = jnp.where(group >= 2, tails[:, 128:], tails[:, :128])
     high, low = tail[:TOP], jnp.concatenate([tail[TOP:], jnp.zeros((2 * TOP - rows, 128), F32)], axis=0)
-    folded = jnp.where(lanes(TOP) < 64, high, pltpu.roll(low, 64, 1))
+    odd = group % 2 == 1
+    folded = jnp.where(
+        lanes(TOP) < 64,
+        jnp.where(odd, pltpu.roll(high, 64, 1), high),
+        jnp.where(odd, low, pltpu.roll(low, 64, 1)),
+    )
     if coded:
         power, gain = scale_of(jnp.maximum(jnp.max(jnp.abs(held[...])), jnp.max(jnp.abs(folded))))
         for n in range(4):
@@ -162,20 +210,20 @@
         out[4 * rows : 4 * rows + TOP, :] = folded
 
 
-def product_group(half, d, spot, left, near, after):
+def product_group(half, d, spot, left, near, tails, after):
     rows = ROWS[half]
     coded = d != 0
     vmem = pl.BlockSpec(memory_space=pltpu.VMEM)
     return pl.pallas_call(
         functools.partial(product_kernel, half, d),
-        in_specs=[pl.BlockSpec(memory_space=pltpu.SMEM), vmem, vmem, pl.BlockSpec(memory_space=pl.ANY)],
+        in_specs=[pl.BlockSpec(memory_space=pltpu.SMEM)] + [vmem] * 3 + [pl.BlockSpec(memory_space=pl.ANY)],
         out_specs=vmem,
         out_shape=jax.ShapeDtypeStruct((4 * rows + TOP, 128), I16 if coded else F32),
         scratch_shapes=[pltpu.VMEM((4, rows, 128), F32)],
-        compiler_params=pltpu.CompilerParams(vmem_limit_bytes=12 * MIB),
-        cost_estimate=pl.CostEstimate(flops=2 * 560 * WIDE * 1024, bytes_accessed=8 * MIB, transcendentals=0),
+        compiler_params=pltpu.CompilerParams(vmem_limit_bytes=10 * MIB),
+        cost_estimate=pl.CostEstimate(flops=2 * 560 * WIDE * 512, bytes_accessed=8 * MIB, transcendentals=0),
         name="product_coded" if coded else "product_own",
-    )(spot, left, near, after)
+    )(spot, left, near, tails, after)
 
 
 def merge_kernel(half, place, own, in1, in2, in3, after, mine, out1, out2, out3, held):
@@ -242,19 +290,20 @@
     spot = jnp.stack([place // 4, place % 4])
     mask = jnp.broadcast_to(jnp.tile(pattern.T, (1, 2))[:, :, None], (16, 16, 128)).astype(BF16)
     blocks_a = jnp.transpose(blocks_a, (0, 2, 1, 3))
-    near = pack_right(jnp.transpose(blocks_b, (0, 2, 1, 3)))
+    near, rest = pack_right(jnp.transpose(blocks_b, (0, 2, 1, 3)))
     after = near
     parts, owns = ([], []), []
     lefts = []
     for half in range(2):
         left = pack_left(half, mask, blocks_a, after)
-        lefts.append(left)
-        after = left
+        tails = product_tails(half, left, rest, after)
+        lefts.append((left, near, tails))
+        after = tails
         for d in (2, 1, 3):
-            after = product_group(half, d, spot, left, near, after)
+            after = product_group(half, d, spot, *lefts[half], after)
             parts[half].append(send(after, half, d))
     for half in range(2):
-        after = product_group(half, 0, spot, lefts[half], near, after)
+        after = product_group(half, 0, spot, *lefts[half], after)
         owns.append(after)
 
     def finish(half, after):
@@ -341,7 +390,7 @@
             flops=2 * count * 256 * 16384, bytes_accessed=(count + 144) * 16384 * 2, transcendentals=0
         ),
         name="collocate",
-    )(keep, ids, own, *parts, basis_cols, basis_rows, *before)
+    )(keep, ids, own, *parts, in_hbm(basis_cols), in_hbm(basis_rows), *before)
 
 
 def bricks_kernel(points, out):

time: 176 us -> 172 us (0.977)
  local copies, waits for them, and re-layouts: 24.4 us -> 13.5 us
  waiting for transfers between devices: 28.3 us -> 35.7 us
    unnamed x45 -> x49, local copies, waits for them, and re-layouts: 23.6 us -> 12.7 us
    pallas_call x8, Pallas kernels: 31.5 us -> 22.8 us  [product_group(): pl.pallas_call(functools.partial(product_kernel, half, d), in_specs=[pl.B...]
    ppermute x12, waiting for transfers between devices: 7.3 us -> 14.7 us  [send(): return lax.ppermute(array, 'col', turn(d, 0) if axis == 0 else turn(0, d))]
    pallas_call x2, Pallas kernels: 9.5 us -> 12.4 us  [pack_left(): pl.pallas_call(functools.partial(pack_left_kernel, count // 2), grid=(ROW...]
    pallas_call x0 -> x2, Pallas kernels: none -> 2.25 us  [product_tails(): pl.pallas_call(functools.partial(tails_kernel, half), in_specs=[vmem] * 3...]
  transfers between devices with their start and end apart: 18 -> 18, of which waited for: 6 -> 8; matrix products, arithmetic and copies ran while one was open for 1% -> 1% of each run, Pallas kernels for 28% -> 22%
where the time goes in v1:
time: 172 us; the launch traced here: 171 us
  Pallas kernels  83.2 us (48%)
  starting transfers between devices  36.5 us (21%)
  waiting for transfers between devices  35.7 us (21%)
  local copies, waits for them, and re-layouts  13.5 us (8%)
    pallas_call x2, Pallas kernels, collocate(): pl.pallas_call(functools.partial(collocate_kernel, half), grid=(16384 //...  25.3 us
    ppermute x12, starting transfers between devices, send(): return lax.ppermute(array, 'col', turn(d, 0) if axis == 0 else turn(0, d))  23 us
    pallas_call x8, Pallas kernels, product_group(): pl.pallas_call(functools.partial(product_kernel, half, d), in_specs=[pl.B...  22.8 us
    ppermute x12, waiting for transfers between devices, send(): return lax.ppermute(array, 'col', turn(d, 0) if axis == 0 else turn(0, d))  14.7 us
    unnamed x49, local copies, waits for them, and re-layouts  12.7 us
    pallas_call x1, Pallas kernels, pack_right(): pl.pallas_call(pack_right_kernel, grid=(8,), in_specs=[pl.BlockSpec((2, B...  12.5 us
    pallas_call x2, Pallas kernels, pack_left(): pl.pallas_call(functools.partial(pack_left_kernel, count // 2), grid=(ROW...  12.4 us
    all_to_all x1, waiting for transfers between devices, shards(): lax.all_to_all(points, 'col', split_axis=0, concat_axis=0, tiled=True)  10.4 us
  transfers between devices with their start and end apart: 18, of which 8 were waited for; matrix products, arithmetic and copies ran while one was open for 1% of the time, Pallas kernels for 22%

profile of v1, /device:TPU:0, one launch (start us, length us, event | category | flops | bytes accessed | tf_op | source)
XLA Modules:
  0.0 171.1 jit_solution(5794684310609586066)
XLA Ops:
  0.7 12.5 %pack_right.1 = (bf16[16,2304,128]{2,1,0:T(8,128)(2,1)S(1)}, bf16[2304,256]{1,0:T(8,128)(2,1)S(1)}) custom-call(bf16[16,138,16,138]{3,2,1,0:T(8,128)(2,1)} %bitcast.41), custom_call_target="tpu_custom_call" | custom-call | flops 16777216 | bytes 31457280 | tf_op jit(solution)/shard_map/pack_right/pallas_call | solution.py:111
  13.2 3.6 %copy-done = bf16[16,2304,128]{2,1,0:T(8,128)(2,1)} copy-done((bf16[16,2304,128]{2,1,0:T(8,128)(2,1)}, bf16[16,2304,128]{2,1,0:T(8,128)(2,1)S(1)}, u32[]{:S(2)}) %copy-start) | copy-done | bytes 9437208
  18.1 3.7 %copy-done.1 = bf16[16,2304,128]{2,1,0:T(8,128)(2,1)S(1)} copy-done((bf16[16,2304,128]{2,1,0:T(8,128)(2,1)S(1)}, bf16[16,2304,128]{2,1,0:T(8,128)(2,1)}, u32[]{:S(2)}) %copy-start.1) | copy-done | bytes 9437208
  21.8 6.4 %pack_left.2.left = bf16[560,2304]{1,0:T(8,128)(2,1)S(1)} custom-call(bf16[16,16,128]{2,1,0:T(8,128)(2,1)S(1)} %broadcast_in_dim.21.mask, bf16[8,138,16,138]{3,2,1,0:T(8,128)(2,1)} %bitcast.39, bf16[16,2304,128]{2,1,0:T(8,128)(2,1)S(1)} %copy-done.1), custom_call_target="tpu_custom_call" | custom-call | flops 16777216 | bytes 7340032 | tf_op jit(solution)/shard_map/pack_left/pallas_call | solution.py:67
  29.1 3.3 %product_coded.6.after = s16[2528,128]{1,0:T(8,128)(2,1)} custom-call(s32[2]{0:T(128)S(1)} %pad_add_fusion.spot.place, bf16[560,2304]{1,0:T(8,128)(2,1)S(1)} %pack_left.2.left, bf16[16,2304,128]{2,1,0:T(8,128)(2,1)S(1)} %copy-done.1, f32[560,256]{1,0:T(8,128)S(1)} %product_tails.2.tails.after, f32[560,256]{1,0:T(8,128)S(1)} %product_tails.2.tails.after), custom_call_target="tpu_custom_call" | custom-call | flops 1321205760 | bytes 8388608 | tf_op jit(solution)/shard_map/product_coded/pallas_call | solution.py:217
  32.4 3.3 %product_coded.7.after = s16[2528,128]{1,0:T(8,128)(2,1)} custom-call(s32[2]{0:T(128)S(1)} %pad_add_fusion.spot.place, bf16[560,2304]{1,0:T(8,128)(2,1)S(1)} %pack_left.2.left, bf16[16,2304,128]{2,1,0:T(8,128)(2,1)S(1)} %copy-done.1, f32[560,256]{1,0:T(8,128)S(1)} %product_tails.2.tails.after, s16[2528,128]{1,0:T(8,128)(2,1)} %product_coded.6.after), custom_call_target="tpu_custom_call" | custom-call | flops 1321205760 | bytes 8388608 | tf_op jit(solution)/shard_map/product_coded/pallas_call | solution.py:217
  35.7 3.3 %product_coded.8.after = s16[2528,128]{1,0:T(8,128)(2,1)} custom-call(s32[2]{0:T(128)S(1)} %pad_add_fusion.spot.place, bf16[560,2304]{1,0:T(8,128)(2,1)S(1)} %pack_left.2.left, bf16[16,2304,128]{2,1,0:T(8,128)(2,1)S(1)} %copy-done.1, f32[560,256]{1,0:T(8,128)S(1)} %product_tails.2.tails.after, s16[2528,128]{1,0:T(8,128)(2,1)} %product_coded.7.after), custom_call_target="tpu_custom_call" | custom-call | flops 1321205760 | bytes 8388608 | tf_op jit(solution)/shard_map/product_coded/pallas_call | solution.py:217
  39.0 3.1 %collective-permute-start.2 = (s16[2528,128]{1,0:T(8,128)(2,1)}, s16[2528,128]{1,0:T(8,128)(2,1)}, u32[]{:S(2)}, u32[]{:S(2)}) collective-permute-start(s16[2528,128]{1,0:T(8,128)(2,1)} %product_coded.8.after), channel_id=1, source_target_pairs={{0,12},{1,13},{2,14},{3,15},{4,0},{5,1},{6,2},{7,3},{8,4},{9,5},{1... | collective-permute-start | bytes 1941512 | tf_op jit(solution)/shard_map/ppermute | solution.py:285
  44.3 6.0 %pack_left.3.left = bf16[544,2304]{1,0:T(8,128)(2,1)S(1)} custom-call(bf16[16,16,128]{2,1,0:T(8,128)(2,1)S(1)} %broadcast_in_dim.21.mask, bf16[8,138,16,138]{3,2,1,0:T(8,128)(2,1)} %bitcast.40, s16[2528,128]{1,0:T(8,128)(2,1)} %product_coded.8.after), custom_call_target="tpu_custom_call" | custom-call | flops 16777216 | bytes 7340032 | tf_op jit(solution)/shard_map/pack_left/pallas_call | solution.py:67
  54.2 3.2 %product_coded.10.after = s16[2464,128]{1,0:T(8,128)(2,1)} custom-call(s32[2]{0:T(128)S(1)} %pad_add_fusion.spot.place, bf16[544,2304]{1,0:T(8,128)(2,1)S(1)} %pack_left.3.left, bf16[16,2304,128]{2,1,0:T(8,128)(2,1)S(1)} %bitcast.33, f32[544,256]{1,0:T(8,128)S(1)} %product_tails.3.tails.after, s16[2464,128]{1,0:T(8,128)(2,1)S(1)} %product_coded.9.after), custom_call_target="tpu_custom_call" | custom-call | flops 1321205760 | bytes 8388608 | tf_op jit(solution)/shard_map/product_coded/pallas_call | solution.py:217
  57.4 3.2 %product_coded.11.after = s16[2464,128]{1,0:T(8,128)(2,1)} custom-call(s32[2]{0:T(128)S(1)} %pad_add_fusion.spot.place, bf16[544,2304]{1,0:T(8,128)(2,1)S(1)} %pack_left.3.left, bf16[16,2304,128]{2,1,0:T(8,128)(2,1)S(1)} %bitcast.33, f32[544,256]{1,0:T(8,128)S(1)} %product_tails.3.tails.after, s16[2464,128]{1,0:T(8,128)(2,1)} %product_coded.10.after), custom_call_target="tpu_custom_call" | custom-call | flops 1321205760 | bytes 8388608 | tf_op jit(solution)/shard_map/product_coded/pallas_call | solution.py:217
  60.7 4.0 %collective-permute-start.8 = (s16[2464,128]{1,0:T(8,128)(2,1)}, s16[2464,128]{1,0:T(8,128)(2,1)}, u32[]{:S(2)}, u32[]{:S(2)}) collective-permute-start(s16[2464,128]{1,0:T(8,128)(2,1)} %product_coded.11.after), channel_id=1, source_target_pairs={{0,3},{1,0},{2,1},{3,2},{4,7},{5,4},{6,5},{7,6},{8,11},{9,8},{10,9... | collective-permute-start | bytes 1892360 | tf_op jit(solution)/shard_map/ppermute | solution.py:285
  64.8 5.3 %collective-permute-done.2.in3 = s16[2528,128]{1,0:T(8,128)(2,1)} collective-permute-done((s16[2528,128]{1,0:T(8,128)(2,1)}, s16[2528,128]{1,0:T(8,128)(2,1)}, u32[]{:S(2)}, u32[]{:S(2)}) %collective-permute-start.2) | collective-permute-done | bytes 647200 | tf_op jit(solution)/shard_map/ppermute | solution.py:285
  70.1 3.9 %collective-permute-start.6 = (s16[2464,128]{1,0:T(8,128)(2,1)}, s16[2464,128]{1,0:T(8,128)(2,1)S(1)}, u32[]{:S(2)}, u32[]{:S(2)}) collective-permute-start(s16[2464,128]{1,0:T(8,128)(2,1)} %copy-done.9), channel_id=1, source_target_pairs={{0,2},{1,3},{2,0},{3,1},{4,6},{5,7},{6,4},{7,5},{8,10},{9,11},{10,... | collective-permute-start | bytes 1892360 | tf_op jit(solution)/shard_map/ppermute | solution.py:285
  74.0 3.7 %copy-done.2 = bf16[16,2304,128]{2,1,0:T(8,128)(2,1)S(1)} copy-done((bf16[16,2304,128]{2,1,0:T(8,128)(2,1)S(1)}, bf16[16,2304,128]{2,1,0:T(8,128)(2,1)}, u32[]{:S(2)}) %copy-start.2) | copy-done | bytes 9437208
  81.8 2.8 %merge.2 = (f32[640,128]{1,0:T(8,128)S(1)}, s16[640,128]{1,0:T(8,128)(2,1)S(1)}, s16[640,128]{1,0:T(8,128)(2,1)S(1)}, s16[640,128]{1,0:T(8,128)(2,1)S(1)}) custom-call(s32[2]{0:T(128)S(1)} %pad_add_fusion.spot.place, f32[2528,128]{1,0:T(8,128)S(1)} %product_own.2.after.own, s16[2528,128]{1,0:T(8,128)(2,1)} %collective-permute-done.in1, ...), custom_call_target="tpu_custom_call" | custom-call | flops 4194304 | bytes 4194304 | tf_op jit(solution)/shard_map/merge/pallas_call | solution.py:268
  86.3 8.5 %collective-permute-done.8.in3 = s16[2464,128]{1,0:T(8,128)(2,1)} collective-permute-done((s16[2464,128]{1,0:T(8,128)(2,1)}, s16[2464,128]{1,0:T(8,128)(2,1)}, u32[]{:S(2)}, u32[]{:S(2)}) %collective-permute-start.8) | collective-permute-done | bytes 630816 | tf_op jit(solution)/shard_map/ppermute | solution.py:285
  94.7 3.7 %collective-permute-start.5 = (s16[640,128]{1,0:T(8,128)(2,1)S(1)}, s16[640,128]{1,0:T(8,128)(2,1)S(1)}, u32[]{:S(2)}, u32[]{:S(2)}) collective-permute-start(s16[640,128]{1,0:T(8,128)(2,1)S(1)} %get-tuple-element.21), channel_id=1, source_target_pairs={{0,3},{1,0},{2,1},{3,2},{4,7},{5,4},{6,5},{7,6},{8,11},{9,8},{10,9... | collective-permute-start | bytes 491528 | tf_op jit(solution)/shard_map/ppermute | solution.py:285
  106.5 12.4 %collocate.2 = (bf16[70,8,138]{2,1,0:T(8,128)(2,1)S(1)}, f32[16,8,1024]{2,1,0:T(8,128)S(1)}) custom-call(f32[8,128]{1,0:T(8,128)S(1)} %broadcast_in_dim.20.keep, f32[8,128]{1,0:T(8,128)S(1)} %concatenate.6.ids, f32[640,128]{1,0:T(8,128)S(1)} %get-tuple-element.18.own.after, s16[640,128]{1,0:T(8,128)(2,1)S(1)} %collective-permute-done.3.in1, ...), custom_call_target="tpu_custom_call" | custom-call | flops 4697620480 | bytes 23068672 | tf_op jit(solution)/shard_map/collocate/pallas_call | solution.py:367
  118.9 12.9 %collocate.3 = (bf16[68,8,138]{2,1,0:T(8,128)(2,1)S(1)}, f32[16,8,1152]{2,1,0:T(8,128)}) custom-call(f32[8,128]{1,0:T(8,128)S(1)} %broadcast_in_dim.20.keep, f32[8,128]{1,0:T(8,128)S(1)} %concatenate.6.ids, f32[624,128]{1,0:T(8,128)S(1)} %get-tuple-element.23.own, s16[624,128]{1,0:T(8,128)(2,1)S(1)} %collective-permute-done.9.in1, ...), custom_call_target="tpu_custom_call" | custom-call | flops 4563402752 | bytes 22544384 | tf_op jit(solution)/shard_map/collocate/pallas_call | solution.py:367
  131.9 4.1 %all-to-all-start = ((f32[16,8,1152]{2,1,0:T(8,128)}), f32[16,8,1152]{2,1,0:T(8,128)S(1)}, u32[]{:S(2)}, u32[]{:S(2)}) async-start(f32[16,8,1152]{2,1,0:T(8,128)} %get-tuple-element.29), calls=%async_computation | async-start | bytes 1179648 | tf_op jit(solution)/shard_map/all_to_all | solution.py:489
  136.0 10.4 %all-to-all-done.points = f32[16,8,1152]{2,1,0:T(8,128)S(1)} async-done(((f32[16,8,1152]{2,1,0:T(8,128)}), f32[16,8,1152]{2,1,0:T(8,128)S(1)}, u32[]{:S(2)}, u32[]{:S(2)}) %all-to-all-start) | async-done | bytes 589856 | tf_op jit(solution)/shard_map/all_to_all | solution.py:489
  159.4 3.5 %all-to-all-start.1 = ((f32[16,8,128]{2,1,0:T(8,128)}), f32[16,8,128]{2,1,0:T(8,128)S(1)}, u32[]{:S(2)}, u32[]{:S(2)}) async-start(f32[16,8,128]{2,1,0:T(8,128)} %filter_rows.1), calls=%async_computation.1 | async-start | bytes 131072 | tf_op jit(solution)/shard_map/all_to_all | solution.py:492
  163.8 6.7 %all-to-all-done.1 = f32[16,8,128]{2,1,0:T(8,128)S(1)} async-done(((f32[16,8,128]{2,1,0:T(8,128)}), f32[16,8,128]{2,1,0:T(8,128)S(1)}, u32[]{:S(2)}, u32[]{:S(2)}) %all-to-all-start.1) | async-done | bytes 65568 | tf_op jit(solution)/shard_map/all_to_all | solution.py:492
  (98 shorter events, 36.4 us)
Async XLA Ops:
  39.0 31.1 %collective-permute-start.2 = (s16[2528,128]{1,0:T(8,128)(2,1)}, s16[2528,128]{1,0:T(8,128)(2,1)}, u32[]{:S(2)}, u32[]{:S(2)}) collective-permute-start(s16[2528,128]{1,0:T(8,128)(2,1)} %product_coded.8.after), channel_id=1, source_target_pairs={{0,12},{1,13},{2,14},{3,15},{4,0},{5,1},{6,2},{7,3},{8,4},{9,5},{1... | collective-permute-start | bytes 1941512 | tf_op jit(solution)/shard_map/ppermute | solution.py:285
  42.1 39.7 %collective-permute-start.1 = (s16[2528,128]{1,0:T(8,128)(2,1)}, s16[2528,128]{1,0:T(8,128)(2,1)}, u32[]{:S(2)}, u32[]{:S(2)}) collective-permute-start(s16[2528,128]{1,0:T(8,128)(2,1)} %product_coded.7.after), channel_id=1, source_target_pairs={{0,4},{1,5},{2,6},{3,7},{4,8},{5,9},{6,10},{7,11},{8,12},{9,13},{1... | collective-permute-start | bytes 1941512 | tf_op jit(solution)/shard_map/ppermute | solution.py:285
  42.1 39.7 %collective-permute-start = (s16[2528,128]{1,0:T(8,128)(2,1)}, s16[2528,128]{1,0:T(8,128)(2,1)}, u32[]{:S(2)}, u32[]{:S(2)}) collective-permute-start(s16[2528,128]{1,0:T(8,128)(2,1)} %product_coded.6.after), channel_id=1, source_target_pairs={{0,8},{1,9},{2,10},{3,11},{4,12},{5,13},{6,14},{7,15},{8,0},{9,1},... | collective-permute-start | bytes 1941512 | tf_op jit(solution)/shard_map/ppermute | solution.py:285
  60.7 34.0 %collective-permute-start.8 = (s16[2464,128]{1,0:T(8,128)(2,1)}, s16[2464,128]{1,0:T(8,128)(2,1)}, u32[]{:S(2)}, u32[]{:S(2)}) collective-permute-start(s16[2464,128]{1,0:T(8,128)(2,1)} %product_coded.11.after), channel_id=1, source_target_pairs={{0,3},{1,0},{2,1},{3,2},{4,7},{5,4},{6,5},{7,6},{8,11},{9,8},{10,9... | collective-permute-start | bytes 1892360 | tf_op jit(solution)/shard_map/ppermute | solution.py:285
  64.7 34.6 %collective-permute-start.7 = (s16[2464,128]{1,0:T(8,128)(2,1)}, s16[2464,128]{1,0:T(8,128)(2,1)}, u32[]{:S(2)}, u32[]{:S(2)}) collective-permute-start(s16[2464,128]{1,0:T(8,128)(2,1)} %product_coded.10.after), channel_id=1, source_target_pairs={{0,1},{1,2},{2,3},{3,0},{4,5},{5,6},{6,7},{7,4},{8,9},{9,10},{10,1... | collective-permute-start | bytes 1892360 | tf_op jit(solution)/shard_map/ppermute | solution.py:285
  70.1 29.2 %collective-permute-start.6 = (s16[2464,128]{1,0:T(8,128)(2,1)}, s16[2464,128]{1,0:T(8,128)(2,1)S(1)}, u32[]{:S(2)}, u32[]{:S(2)}) collective-permute-start(s16[2464,128]{1,0:T(8,128)(2,1)} %copy-done.9), channel_id=1, source_target_pairs={{0,2},{1,3},{2,0},{3,1},{4,6},{5,7},{6,4},{7,5},{8,10},{9,11},{10,... | collective-permute-start | bytes 1892360 | tf_op jit(solution)/shard_map/ppermute | solution.py:285
  84.6 20.6 %collective-permute-start.3 = (s16[640,128]{1,0:T(8,128)(2,1)S(1)}, s16[640,128]{1,0:T(8,128)(2,1)S(1)}, u32[]{:S(2)}, u32[]{:S(2)}) collective-permute-start(s16[640,128]{1,0:T(8,128)(2,1)S(1)} %get-tuple-element.19), channel_id=1, source_target_pairs={{0,2},{1,3},{2,0},{3,1},{4,6},{5,7},{6,4},{7,5},{8,10},{9,11},{10,... | collective-permute-start | bytes 491528 | tf_op jit(solution)/shard_map/ppermute | solution.py:285
  84.7 21.7 %collective-permute-start.4 = (s16[640,128]{1,0:T(8,128)(2,1)S(1)}, s16[640,128]{1,0:T(8,128)(2,1)S(1)}, u32[]{:S(2)}, u32[]{:S(2)}) collective-permute-start(s16[640,128]{1,0:T(8,128)(2,1)S(1)} %get-tuple-element.20), channel_id=1, source_target_pairs={{0,1},{1,2},{2,3},{3,0},{4,5},{5,6},{6,7},{7,4},{8,9},{9,10},{10,1... | collective-permute-start | bytes 491528 | tf_op jit(solution)/shard_map/ppermute | solution.py:285
  94.7 11.7 %collective-permute-start.5 = (s16[640,128]{1,0:T(8,128)(2,1)S(1)}, s16[640,128]{1,0:T(8,128)(2,1)S(1)}, u32[]{:S(2)}, u32[]{:S(2)}) collective-permute-start(s16[640,128]{1,0:T(8,128)(2,1)S(1)} %get-tuple-element.21), channel_id=1, source_target_pairs={{0,3},{1,0},{2,1},{3,2},{4,7},{5,4},{6,5},{7,6},{8,11},{9,8},{10,9... | collective-permute-start | bytes 491528 | tf_op jit(solution)/shard_map/ppermute | solution.py:285
  101.9 17.0 %collective-permute-start.10 = (s16[624,128]{1,0:T(8,128)(2,1)S(1)}, s16[624,128]{1,0:T(8,128)(2,1)S(1)}, u32[]{:S(2)}, u32[]{:S(2)}) collective-permute-start(s16[624,128]{1,0:T(8,128)(2,1)S(1)} %get-tuple-element.25), channel_id=1, source_target_pairs={{0,4},{1,5},{2,6},{3,7},{4,8},{5,9},{6,10},{7,11},{8,12},{9,13},{1... | collective-permute-start | bytes 479240 | tf_op jit(solution)/shard_map/ppermute | solution.py:285
  104.3 14.6 %collective-permute-start.11 = (s16[624,128]{1,0:T(8,128)(2,1)S(1)}, s16[624,128]{1,0:T(8,128)(2,1)S(1)}, u32[]{:S(2)}, u32[]{:S(2)}) collective-permute-start(s16[624,128]{1,0:T(8,128)(2,1)S(1)} %get-tuple-element.26), channel_id=1, source_target_pairs={{0,12},{1,13},{2,14},{3,15},{4,0},{5,1},{6,2},{7,3},{8,4},{9,5},{1... | collective-permute-start | bytes 479240 | tf_op jit(solution)/shard_map/ppermute | solution.py:285
  105.2 13.7 %collective-permute-start.9 = (s16[624,128]{1,0:T(8,128)(2,1)S(1)}, s16[624,128]{1,0:T(8,128)(2,1)S(1)}, u32[]{:S(2)}, u32[]{:S(2)}) collective-permute-start(s16[624,128]{1,0:T(8,128)(2,1)S(1)} %get-tuple-element.24), channel_id=1, source_target_pairs={{0,8},{1,9},{2,10},{3,11},{4,12},{5,13},{6,14},{7,15},{8,0},{9,1},... | collective-permute-start | bytes 479240 | tf_op jit(solution)/shard_map/ppermute | solution.py:285
  118.9 35.7 %copy-start.17 = (f32[8,2048]{1,0:T(8,128)S(1)}, f32[8,2048]{1,0:T(8,128)}, u32[]{:S(2)}) copy-start(f32[8,2048]{1,0:T(8,128)} %param.23) | copy-start | bytes 196612
  131.8 25.6 %copy-start.11 = (f32[256,256]{1,0:T(8,128)S(1)}, f32[256,256]{1,0:T(8,128)}, u32[]{:S(2)}) copy-start(f32[256,256]{1,0:T(8,128)} %constant.115.clone.second) | copy-start | bytes 786436
  131.8 25.6 %copy-start.12 = (f32[256,256]{1,0:T(8,128)S(1)}, f32[256,256]{1,0:T(8,128)}, u32[]{:S(2)}) copy-start(f32[256,256]{1,0:T(8,128)} %constant.116.clone.third) | copy-start | bytes 786436
  131.8 25.6 %copy-start.13 = (f32[256,128]{1,0:T(8,128)S(1)}, f32[256,128]{1,0:T(8,128)}, u32[]{:S(2)}) copy-start(f32[256,128]{1,0:T(8,128)} %constant.114.clone.first) | copy-start | bytes 393220
  131.8 25.6 %copy-start.14 = (f32[128,256]{1,0:T(8,128)S(1)}, f32[128,256]{1,0:T(8,128)}, u32[]{:S(2)}) copy-start(f32[128,256]{1,0:T(8,128)} %constant.117.clone.last) | copy-start | bytes 393220
  131.8 25.6 %copy-start.15 = (f32[128,128]{1,0:T(8,128)S(1)}, f32[128,128]{1,0:T(8,128)}, u32[]{:S(2)}) copy-start(f32[128,128]{1,0:T(8,128)} %constant.118.clone.tc) | copy-start | bytes 196612
  131.9 14.5 %all-to-all-start = ((f32[16,8,1152]{2,1,0:T(8,128)}), f32[16,8,1152]{2,1,0:T(8,128)S(1)}, u32[]{:S(2)}, u32[]{:S(2)}) async-start(f32[16,8,1152]{2,1,0:T(8,128)} %get-tuple-element.29), calls=%async_computation | async-start | bytes 1179648 | tf_op jit(solution)/shard_map/all_to_all | solution.py:489
  147.0 1.6 collective-permute-start.12
  148.7 6.2 %collective-permute-start.13 = (f32[16,1024]{1,0:T(8,128)S(1)}, f32[16,1024]{1,0:T(8,128)S(1)}, u32[]{:S(2)}, u32[]{:S(2)}) collective-permute-start(f32[16,1024]{1,0:T(8,128)S(1)} %get-tuple-element.32), channel_id=1, source_target_pairs={{0,32},{16,48},{32,64},{48,80},{64,96},{80,112},{96,0},{112,16},{1... | collective-permute-start | bytes 196616 | tf_op jit(solution)/shard_map/ppermute | solution.py:468
  150.4 6.2 %collective-permute-start.14 = (f32[16,1024]{1,0:T(8,128)S(1)}, f32[16,1024]{1,0:T(8,128)S(1)}, u32[]{:S(2)}, u32[]{:S(2)}) collective-permute-start(f32[16,1024]{1,0:T(8,128)S(1)} %get-tuple-element.31), channel_id=1, source_target_pairs={{0,64},{16,80},{32,96},{48,112},{64,0},{80,16},{96,32},{112,48},{1... | collective-permute-start | bytes 196616 | tf_op jit(solution)/shard_map/ppermute | solution.py:468
  153.1 4.3 %collective-permute-start.15 = (f32[16,1024]{1,0:T(8,128)S(1)}, f32[16,1024]{1,0:T(8,128)S(1)}, u32[]{:S(2)}, u32[]{:S(2)}) collective-permute-start(f32[16,1024]{1,0:T(8,128)S(1)} %get-tuple-element.30), channel_id=1, source_target_pairs={{0,96},{16,112},{32,0},{48,16},{64,32},{80,48},{96,64},{112,80},{1... | collective-permute-start | bytes 196616 | tf_op jit(solution)/shard_map/ppermute | solution.py:468
  159.4 11.1 %all-to-all-start.1 = ((f32[16,8,128]{2,1,0:T(8,128)}), f32[16,8,128]{2,1,0:T(8,128)S(1)}, u32[]{:S(2)}, u32[]{:S(2)}) async-start(f32[16,8,128]{2,1,0:T(8,128)} %filter_rows.1), calls=%async_computation.1 | async-start | bytes 131072 | tf_op jit(solution)/shard_map/all_to_all | solution.py:492
  (18 other events, 158.5 us)

commit v2 on v1

--- a/solution.py
+++ b/solution.py
@@ -83,7 +83,8 @@
     )(mask, in_hbm(blocks), after)
 
 
-def pack_right_kernel(blocks, near, rest):
+def pack_right_kernel(blocks, *others):
+    near, rest = others[-2:]
     base = pl.program_id(0) % 4 * 2
 
     def step(n, carry):
@@ -107,11 +108,12 @@
     lax.fori_loop(0, 2, step, 0)
 
 
-def pack_right(blocks):
+def pack_right(blocks, before):
     return pl.pallas_call(
         pack_right_kernel,
         grid=(8,),
-        in_specs=[pl.BlockSpec((2, BS, 16, BS), lambda g: (g, 0, 0, 0))],
+        in_specs=[pl.BlockSpec((2, BS, 16, BS), lambda g: (g, 0, 0, 0))]
+        + [pl.BlockSpec(memory_space=pl.ANY)] * len(before),
         out_specs=[
             pl.BlockSpec((16, SPAN, 128), lambda g: (0, g // 4, 0)),
             pl.BlockSpec((SPAN, 256), lambda g: (g // 4, 0)),
@@ -123,7 +125,7 @@
         compiler_params=pltpu.CompilerParams(vmem_limit_bytes=24 * MIB),
         cost_estimate=pl.CostEstimate(flops=1 << 24, bytes_accessed=30 * MIB, transcendentals=0),
         name="pack_right",
-    )(in_hbm(blocks))
+    )(in_hbm(blocks), *before)
 
 
 def tails_kernel(half, left, rest, swap, after, out):
@@ -285,12 +287,12 @@
     return lax.ppermute(array, "col", turn(d, 0) if axis == 0 else turn(0, d))
 
 
-def exchange_products(blocks_a, pattern, blocks_b):
+def exchange_products(blocks_a, pattern, blocks_b, before):
     place = lax.axis_index("col").astype(jnp.int32)
     spot = jnp.stack([place // 4, place % 4])
     mask = jnp.broadcast_to(jnp.tile(pattern.T, (1, 2))[:, :, None], (16, 16, 128)).astype(BF16)
     blocks_a = jnp.transpose(blocks_a, (0, 2, 1, 3))
-    near, rest = pack_right(jnp.transpose(blocks_b, (0, 2, 1, 3)))
+    near, rest = pack_right(jnp.transpose(blocks_b, (0, 2, 1, 3)), [mask, spot] + before)
     after = near
     parts, owns = ([], []), []
     lefts = []
@@ -476,7 +478,7 @@
     ids = jnp.concatenate([owners.astype(F32)[None], jnp.zeros((7, 128), F32)], axis=0)
     keep = jnp.broadcast_to(filter_mask.reshape(8, 1).astype(F32), (8, 128))
     by_point = jnp.transpose(basis_rows, (1, 0, 2))
-    finish, after = exchange_products(blocks_a, pattern_a, blocks_b)
+    finish, after = exchange_products(blocks_a, pattern_a, blocks_b, [kern, ids, keep])
     densities, before, sums = [], [], []
     for half in range(2):
         sums.append(finish(half, after))

time: 172 us -> 162 us (0.942)
  local copies, waits for them, and re-layouts: 13.5 us -> 2.95 us
  Pallas kernels: 83.2 us -> 77.2 us
  waiting for transfers between devices: 35.7 us -> 40.6 us
    unnamed x49 -> x15, local copies, waits for them, and re-layouts: 12.7 us -> 0.68 us
    ppermute x12, waiting for transfers between devices: 14.7 us -> 19.2 us  [send(): return lax.ppermute(array, 'col', turn(d, 0) if axis == 0 else turn(0, d))]
    pallas_call x8, Pallas kernels: 22.8 us -> 18.6 us  [product_group(): pl.pallas_call(functools.partial(product_kernel, half, d), in_specs=[pl.B...]
where the time goes in v2:
time: 162 us; the launch traced here: 161 us
  Pallas kernels  77.2 us (48%)
  waiting for transfers between devices  40.6 us (25%)
  starting transfers between devices  36.5 us (23%)
  local copies, waits for them, and re-layouts  2.95 us (2%)
  other arithmetic  2.37 us (1%)
    pallas_call x2, Pallas kernels, collocate(): pl.pallas_call(functools.partial(collocate_kernel, half), grid=(16384 //...  25.3 us
    ppermute x12, starting transfers between devices, send(): return lax.ppermute(array, 'col', turn(d, 0) if axis == 0 else turn(0, d))  23.3 us
    ppermute x12, waiting for transfers between devices, send(): return lax.ppermute(array, 'col', turn(d, 0) if axis == 0 else turn(0, d))  19.2 us
    pallas_call x8, Pallas kernels, product_group(): pl.pallas_call(functools.partial(product_kernel, half, d), in_specs=[pl.B...  18.6 us
    pallas_call x1, Pallas kernels, pack_right(): pl.pallas_call(pack_right_kernel, grid=(8,), in_specs=[pl.BlockSpec((2, B...  12.5 us
    pallas_call x2, Pallas kernels, pack_left(): pl.pallas_call(functools.partial(pack_left_kernel, count // 2), grid=(ROW...  12.3 us
    all_to_all x1, waiting for transfers between devices, shards(): lax.all_to_all(points, 'col', split_axis=0, concat_axis=0, tiled=True)  10.4 us
    all_to_all x1, waiting for transfers between devices, shards(): lax.all_to_all(filtered, 'col', split_axis=0, concat_axis=0, tiled=True)  6.71 us
  transfers between devices with their start and end apart: 18, of which 8 were waited for; matrix products, arithmetic and copies ran while one was open for 1% of the time, Pallas kernels for 22%

profile of v2, /device:TPU:0, one launch (start us, length us, event | category | flops | bytes accessed | tf_op | source)
XLA Modules:
  0.0 160.7 jit_solution(4923973746180500016)
XLA Ops:
  4.3 12.5 %pack_right.1 = (bf16[16,2304,128]{2,1,0:T(8,128)(2,1)S(1)}, bf16[2304,256]{1,0:T(8,128)(2,1)S(1)}) custom-call(bf16[16,138,16,138]{3,2,1,0:T(8,128)(2,1)} %bitcast.40, bf16[16,16,128]{2,1,0:T(8,128)(2,1)S(1)} %broadcast_in_dim.21.others_0_.mask, s32[2]{0:T(128)S(1)} %pad_add_fusion.others_1_.spot.place, f32[128,128]{1,0:T(8,128)S(1)} %bitcast.34, ...), custom_call_target="tpu_custom_call" | custom-call | flops 16777216 | bytes 31457280 | tf_op jit(solution)/shard_map/pack_right/pallas_call | solution.py:112
  16.9 6.3 %pack_left.2.left = bf16[560,2304]{1,0:T(8,128)(2,1)S(1)} custom-call(bf16[16,16,128]{2,1,0:T(8,128)(2,1)S(1)} %broadcast_in_dim.21.others_0_.mask, bf16[8,138,16,138]{3,2,1,0:T(8,128)(2,1)} %bitcast.38, bf16[16,2304,128]{2,1,0:T(8,128)(2,1)S(1)} %get-tuple-element.16.after.near), custom_call_target="tpu_custom_call" | custom-call | flops 16777216 | bytes 7340032 | tf_op jit(solution)/shard_map/pack_left/pallas_call | solution.py:67
  24.0 2.4 %product_coded.6.after = s16[2528,128]{1,0:T(8,128)(2,1)S(1)} custom-call(s32[2]{0:T(128)S(1)} %pad_add_fusion.others_1_.spot.place, bf16[560,2304]{1,0:T(8,128)(2,1)S(1)} %pack_left.2.left, bf16[16,2304,128]{2,1,0:T(8,128)(2,1)S(1)} %get-tuple-element.16.after.near, f32[560,256]{1,0:T(8,128)S(1)} %product_tails.2.tails.after, ...), custom_call_target="tpu_custom_call" | custom-call | flops 1321205760 | bytes 8388608 | tf_op jit(solution)/shard_map/product_coded/pallas_call | solution.py:219
  26.5 2.4 %product_coded.7.after = s16[2528,128]{1,0:T(8,128)(2,1)S(1)} custom-call(s32[2]{0:T(128)S(1)} %pad_add_fusion.others_1_.spot.place, bf16[560,2304]{1,0:T(8,128)(2,1)S(1)} %pack_left.2.left, bf16[16,2304,128]{2,1,0:T(8,128)(2,1)S(1)} %get-tuple-element.16.after.near, f32[560,256]{1,0:T(8,128)S(1)} %product_tails.2.tails.after, ...), custom_call_target="tpu_custom_call" | custom-call | flops 1321205760 | bytes 8388608 | tf_op jit(solution)/shard_map/product_coded/pallas_call | solution.py:219
  28.9 2.4 %product_coded.8.after = s16[2528,128]{1,0:T(8,128)(2,1)S(1)} custom-call(s32[2]{0:T(128)S(1)} %pad_add_fusion.others_1_.spot.place, bf16[560,2304]{1,0:T(8,128)(2,1)S(1)} %pack_left.2.left, bf16[16,2304,128]{2,1,0:T(8,128)(2,1)S(1)} %get-tuple-element.16.after.near, f32[560,256]{1,0:T(8,128)S(1)} %product_tails.2.tails.after, ...), custom_call_target="tpu_custom_call" | custom-call | flops 1321205760 | bytes 8388608 | tf_op jit(solution)/shard_map/product_coded/pallas_call | solution.py:219
  31.4 3.2 %collective-permute-start.2 = (s16[2528,128]{1,0:T(8,128)(2,1)S(1)}, s16[2528,128]{1,0:T(8,128)(2,1)S(1)}, u32[]{:S(2)}, u32[]{:S(2)}) collective-permute-start(s16[2528,128]{1,0:T(8,128)(2,1)S(1)} %product_coded.8.after), channel_id=1, source_target_pairs={{0,12},{1,13},{2,14},{3,15},{4,0},{5,1},{6,2},{7,3},{8,4},{9,5},{1... | collective-permute-start | bytes 1941512 | tf_op jit(solution)/shard_map/ppermute | solution.py:287
  34.6 2.2 %collective-permute-start = (s16[2528,128]{1,0:T(8,128)(2,1)S(1)}, s16[2528,128]{1,0:T(8,128)(2,1)S(1)}, u32[]{:S(2)}, u32[]{:S(2)}) collective-permute-start(s16[2528,128]{1,0:T(8,128)(2,1)S(1)} %product_coded.6.after), channel_id=1, source_target_pairs={{0,8},{1,9},{2,10},{3,11},{4,12},{5,13},{6,14},{7,15},{8,0},{9,1},... | collective-permute-start | bytes 1941512 | tf_op jit(solution)/shard_map/ppermute | solution.py:287
  36.8 6.0 %pack_left.3.left = bf16[544,2304]{1,0:T(8,128)(2,1)S(1)} custom-call(bf16[16,16,128]{2,1,0:T(8,128)(2,1)S(1)} %broadcast_in_dim.21.others_0_.mask, bf16[8,138,16,138]{3,2,1,0:T(8,128)(2,1)} %bitcast.39, s16[2528,128]{1,0:T(8,128)(2,1)S(1)} %product_coded.8.after), custom_call_target="tpu_custom_call" | custom-call | flops 16777216 | bytes 7340032 | tf_op jit(solution)/shard_map/pack_left/pallas_call | solution.py:67
  44.2 2.4 %product_coded.9.after = s16[2464,128]{1,0:T(8,128)(2,1)S(1)} custom-call(s32[2]{0:T(128)S(1)} %pad_add_fusion.others_1_.spot.place, bf16[544,2304]{1,0:T(8,128)(2,1)S(1)} %pack_left.3.left, bf16[16,2304,128]{2,1,0:T(8,128)(2,1)S(1)} %get-tuple-element.16.after.near, f32[544,256]{1,0:T(8,128)S(1)} %product_tails.3.tails.after, ...), custom_call_target="tpu_custom_call" | custom-call | flops 1321205760 | bytes 8388608 | tf_op jit(solution)/shard_map/product_coded/pallas_call | solution.py:219
  46.6 2.4 %product_coded.10.after = s16[2464,128]{1,0:T(8,128)(2,1)S(1)} custom-call(s32[2]{0:T(128)S(1)} %pad_add_fusion.others_1_.spot.place, bf16[544,2304]{1,0:T(8,128)(2,1)S(1)} %pack_left.3.left, bf16[16,2304,128]{2,1,0:T(8,128)(2,1)S(1)} %get-tuple-element.16.after.near, f32[544,256]{1,0:T(8,128)S(1)} %product_tails.3.tails.after, ...), custom_call_target="tpu_custom_call" | custom-call | flops 1321205760 | bytes 8388608 | tf_op jit(solution)/shard_map/product_coded/pallas_call | solution.py:219
  49.0 2.4 %product_coded.11.after = s16[2464,128]{1,0:T(8,128)(2,1)S(1)} custom-call(s32[2]{0:T(128)S(1)} %pad_add_fusion.others_1_.spot.place, bf16[544,2304]{1,0:T(8,128)(2,1)S(1)} %pack_left.3.left, bf16[16,2304,128]{2,1,0:T(8,128)(2,1)S(1)} %get-tuple-element.16.after.near, f32[544,256]{1,0:T(8,128)S(1)} %product_tails.3.tails.after, ...), custom_call_target="tpu_custom_call" | custom-call | flops 1321205760 | bytes 8388608 | tf_op jit(solution)/shard_map/product_coded/pallas_call | solution.py:219
  51.4 4.1 %collective-permute-start.8 = (s16[2464,128]{1,0:T(8,128)(2,1)S(1)}, s16[2464,128]{1,0:T(8,128)(2,1)S(1)}, u32[]{:S(2)}, u32[]{:S(2)}) collective-permute-start(s16[2464,128]{1,0:T(8,128)(2,1)S(1)} %product_coded.11.after), channel_id=1, source_target_pairs={{0,3},{1,0},{2,1},{3,2},{4,7},{5,4},{6,5},{7,6},{8,11},{9,8},{10,9... | collective-permute-start | bytes 1892360 | tf_op jit(solution)/shard_map/ppermute | solution.py:287
  55.5 6.7 %collective-permute-done.2.in3 = s16[2528,128]{1,0:T(8,128)(2,1)S(1)} collective-permute-done((s16[2528,128]{1,0:T(8,128)(2,1)S(1)}, s16[2528,128]{1,0:T(8,128)(2,1)S(1)}, u32[]{:S(2)}, u32[]{:S(2)}) %collective-permute-start.2) | collective-permute-done | bytes 647200 | tf_op jit(solution)/shard_map/ppermute | solution.py:287
  62.2 3.9 %collective-permute-start.6 = (s16[2464,128]{1,0:T(8,128)(2,1)S(1)}, s16[2464,128]{1,0:T(8,128)(2,1)S(1)}, u32[]{:S(2)}, u32[]{:S(2)}) collective-permute-start(s16[2464,128]{1,0:T(8,128)(2,1)S(1)} %product_coded.9.after), channel_id=1, source_target_pairs={{0,2},{1,3},{2,0},{3,1},{4,6},{5,7},{6,4},{7,5},{8,10},{9,11},{10,... | collective-permute-start | bytes 1892360 | tf_op jit(solution)/shard_map/ppermute | solution.py:287
  73.7 11.5 %collective-permute-done.8.in3 = s16[2464,128]{1,0:T(8,128)(2,1)S(1)} collective-permute-done((s16[2464,128]{1,0:T(8,128)(2,1)S(1)}, s16[2464,128]{1,0:T(8,128)(2,1)S(1)}, u32[]{:S(2)}, u32[]{:S(2)}) %collective-permute-start.8) | collective-permute-done | bytes 630816 | tf_op jit(solution)/shard_map/ppermute | solution.py:287
  85.2 3.7 %collective-permute-start.5 = (s16[640,128]{1,0:T(8,128)(2,1)S(1)}, s16[640,128]{1,0:T(8,128)(2,1)S(1)}, u32[]{:S(2)}, u32[]{:S(2)}) collective-permute-start(s16[640,128]{1,0:T(8,128)(2,1)S(1)} %get-tuple-element.21), channel_id=1, source_target_pairs={{0,3},{1,0},{2,1},{3,2},{4,7},{5,4},{6,5},{7,6},{8,11},{9,8},{10,9... | collective-permute-start | bytes 491528 | tf_op jit(solution)/shard_map/ppermute | solution.py:287
  91.6 2.5 %collective-permute-start.10 = (s16[624,128]{1,0:T(8,128)(2,1)S(1)}, s16[624,128]{1,0:T(8,128)(2,1)S(1)}, u32[]{:S(2)}, u32[]{:S(2)}) collective-permute-start(s16[624,128]{1,0:T(8,128)(2,1)S(1)} %get-tuple-element.25), channel_id=1, source_target_pairs={{0,4},{1,5},{2,6},{3,7},{4,8},{5,9},{6,10},{7,11},{8,12},{9,13},{1... | collective-permute-start | bytes 479240 | tf_op jit(solution)/shard_map/ppermute | solution.py:287
  96.3 12.4 %collocate.2 = (bf16[70,8,138]{2,1,0:T(8,128)(2,1)S(1)}, f32[16,8,1024]{2,1,0:T(8,128)S(1)}) custom-call(f32[8,128]{1,0:T(8,128)S(1)} %broadcast_in_dim.20.others_4_.keep, f32[8,128]{1,0:T(8,128)S(1)} %concatenate.6.others_3_.ids, f32[640,128]{1,0:T(8,128)S(1)} %get-tuple-element.18.own.after, s16[640,128]{1,0:T(8,128)(2,1)S(1)} %collective-permute-done.3.in1, ...), custom_call_target="tpu_custom_call" | custom-call | flops 4697620480 | bytes 23068672 | tf_op jit(solution)/shard_map/collocate/pallas_call | solution.py:369
  108.8 13.0 %collocate.3 = (bf16[68,8,138]{2,1,0:T(8,128)(2,1)S(1)}, f32[16,8,1152]{2,1,0:T(8,128)}) custom-call(f32[8,128]{1,0:T(8,128)S(1)} %broadcast_in_dim.20.others_4_.keep, f32[8,128]{1,0:T(8,128)S(1)} %concatenate.6.others_3_.ids, f32[624,128]{1,0:T(8,128)S(1)} %get-tuple-element.23.own, s16[624,128]{1,0:T(8,128)(2,1)S(1)} %collective-permute-done.9.in1, ...), custom_call_target="tpu_custom_call" | custom-call | flops 4563402752 | bytes 22544384 | tf_op jit(solution)/shard_map/collocate/pallas_call | solution.py:369
  121.8 3.9 %all-to-all-start = ((f32[16,8,1152]{2,1,0:T(8,128)}), f32[16,8,1152]{2,1,0:T(8,128)S(1)}, u32[]{:S(2)}, u32[]{:S(2)}) async-start(f32[16,8,1152]{2,1,0:T(8,128)} %get-tuple-element.29), calls=%async_computation | async-start | bytes 1179648 | tf_op jit(solution)/shard_map/all_to_all | solution.py:491
  125.7 10.4 %all-to-all-done.points = f32[16,8,1152]{2,1,0:T(8,128)S(1)} async-done(((f32[16,8,1152]{2,1,0:T(8,128)}), f32[16,8,1152]{2,1,0:T(8,128)S(1)}, u32[]{:S(2)}, u32[]{:S(2)}) %all-to-all-start) | async-done | bytes 589856 | tf_op jit(solution)/shard_map/all_to_all | solution.py:491
  140.0 2.7 %collective-permute-start.14 = (f32[16,1024]{1,0:T(8,128)S(1)}, f32[16,1024]{1,0:T(8,128)S(1)}, u32[]{:S(2)}, u32[]{:S(2)}) collective-permute-start(f32[16,1024]{1,0:T(8,128)S(1)} %get-tuple-element.31), channel_id=1, source_target_pairs={{0,64},{16,80},{32,96},{48,112},{64,0},{80,16},{96,32},{112,48},{1... | collective-permute-start | bytes 196616 | tf_op jit(solution)/shard_map/ppermute | solution.py:470
  149.0 3.5 %all-to-all-start.1 = ((f32[16,8,128]{2,1,0:T(8,128)}), f32[16,8,128]{2,1,0:T(8,128)S(1)}, u32[]{:S(2)}, u32[]{:S(2)}) async-start(f32[16,8,128]{2,1,0:T(8,128)} %filter_rows.1), calls=%async_computation.1 | async-start | bytes 131072 | tf_op jit(solution)/shard_map/all_to_all | solution.py:494
  153.4 6.7 %all-to-all-done.1 = f32[16,8,128]{2,1,0:T(8,128)S(1)} async-done(((f32[16,8,128]{2,1,0:T(8,128)}), f32[16,8,128]{2,1,0:T(8,128)S(1)}, u32[]{:S(2)}, u32[]{:S(2)}) %all-to-all-start.1) | async-done | bytes 65568 | tf_op jit(solution)/shard_map/all_to_all | solution.py:494
  (63 shorter events, 29.9 us)
Async XLA Ops:
  31.4 30.9 %collective-permute-start.2 = (s16[2528,128]{1,0:T(8,128)(2,1)S(1)}, s16[2528,128]{1,0:T(8,128)(2,1)S(1)}, u32[]{:S(2)}, u32[]{:S(2)}) collective-permute-start(s16[2528,128]{1,0:T(8,128)(2,1)S(1)} %product_coded.8.after), channel_id=1, source_target_pairs={{0,12},{1,13},{2,14},{3,15},{4,0},{5,1},{6,2},{7,3},{8,4},{9,5},{1... | collective-permute-start | bytes 1941512 | tf_op jit(solution)/shard_map/ppermute | solution.py:287
  34.6 35.6 %collective-permute-start.1 = (s16[2528,128]{1,0:T(8,128)(2,1)S(1)}, s16[2528,128]{1,0:T(8,128)(2,1)S(1)}, u32[]{:S(2)}, u32[]{:S(2)}) collective-permute-start(s16[2528,128]{1,0:T(8,128)(2,1)S(1)} %product_coded.7.after), channel_id=1, source_target_pairs={{0,4},{1,5},{2,6},{3,7},{4,8},{5,9},{6,10},{7,11},{8,12},{9,13},{1... | collective-permute-start | bytes 1941512 | tf_op jit(solution)/shard_map/ppermute | solution.py:287
  34.6 35.6 %collective-permute-start = (s16[2528,128]{1,0:T(8,128)(2,1)S(1)}, s16[2528,128]{1,0:T(8,128)(2,1)S(1)}, u32[]{:S(2)}, u32[]{:S(2)}) collective-permute-start(s16[2528,128]{1,0:T(8,128)(2,1)S(1)} %product_coded.6.after), channel_id=1, source_target_pairs={{0,8},{1,9},{2,10},{3,11},{4,12},{5,13},{6,14},{7,15},{8,0},{9,1},... | collective-permute-start | bytes 1941512 | tf_op jit(solution)/shard_map/ppermute | solution.py:287
  51.4 33.8 %collective-permute-start.8 = (s16[2464,128]{1,0:T(8,128)(2,1)S(1)}, s16[2464,128]{1,0:T(8,128)(2,1)S(1)}, u32[]{:S(2)}, u32[]{:S(2)}) collective-permute-start(s16[2464,128]{1,0:T(8,128)(2,1)S(1)} %product_coded.11.after), channel_id=1, source_target_pairs={{0,3},{1,0},{2,1},{3,2},{4,7},{5,4},{6,5},{7,6},{8,11},{9,8},{10,9... | collective-permute-start | bytes 1892360 | tf_op jit(solution)/shard_map/ppermute | solution.py:287
  55.5 34.3 %collective-permute-start.7 = (s16[2464,128]{1,0:T(8,128)(2,1)S(1)}, s16[2464,128]{1,0:T(8,128)(2,1)S(1)}, u32[]{:S(2)}, u32[]{:S(2)}) collective-permute-start(s16[2464,128]{1,0:T(8,128)(2,1)S(1)} %product_coded.10.after), channel_id=1, source_target_pairs={{0,1},{1,2},{2,3},{3,0},{4,5},{5,6},{6,7},{7,4},{8,9},{9,10},{10,1... | collective-permute-start | bytes 1892360 | tf_op jit(solution)/shard_map/ppermute | solution.py:287
  62.2 27.5 %collective-permute-start.6 = (s16[2464,128]{1,0:T(8,128)(2,1)S(1)}, s16[2464,128]{1,0:T(8,128)(2,1)S(1)}, u32[]{:S(2)}, u32[]{:S(2)}) collective-permute-start(s16[2464,128]{1,0:T(8,128)(2,1)S(1)} %product_coded.9.after), channel_id=1, source_target_pairs={{0,2},{1,3},{2,0},{3,1},{4,6},{5,7},{6,4},{7,5},{8,10},{9,11},{10,... | collective-permute-start | bytes 1892360 | tf_op jit(solution)/shard_map/ppermute | solution.py:287
  72.1 22.9 %collective-permute-start.3 = (s16[640,128]{1,0:T(8,128)(2,1)S(1)}, s16[640,128]{1,0:T(8,128)(2,1)S(1)}, u32[]{:S(2)}, u32[]{:S(2)}) collective-permute-start(s16[640,128]{1,0:T(8,128)(2,1)S(1)} %get-tuple-element.19), channel_id=1, source_target_pairs={{0,2},{1,3},{2,0},{3,1},{4,6},{5,7},{6,4},{7,5},{8,10},{9,11},{10,... | collective-permute-start | bytes 491528 | tf_op jit(solution)/shard_map/ppermute | solution.py:287
  72.2 24.1 %collective-permute-start.4 = (s16[640,128]{1,0:T(8,128)(2,1)S(1)}, s16[640,128]{1,0:T(8,128)(2,1)S(1)}, u32[]{:S(2)}, u32[]{:S(2)}) collective-permute-start(s16[640,128]{1,0:T(8,128)(2,1)S(1)} %get-tuple-element.20), channel_id=1, source_target_pairs={{0,1},{1,2},{2,3},{3,0},{4,5},{5,6},{6,7},{7,4},{8,9},{9,10},{10,1... | collective-permute-start | bytes 491528 | tf_op jit(solution)/shard_map/ppermute | solution.py:287
  85.2 11.1 %collective-permute-start.5 = (s16[640,128]{1,0:T(8,128)(2,1)S(1)}, s16[640,128]{1,0:T(8,128)(2,1)S(1)}, u32[]{:S(2)}, u32[]{:S(2)}) collective-permute-start(s16[640,128]{1,0:T(8,128)(2,1)S(1)} %get-tuple-element.21), channel_id=1, source_target_pairs={{0,3},{1,0},{2,1},{3,2},{4,7},{5,4},{6,5},{7,6},{8,11},{9,8},{10,9... | collective-permute-start | bytes 491528 | tf_op jit(solution)/shard_map/ppermute | solution.py:287
  91.6 17.0 %collective-permute-start.10 = (s16[624,128]{1,0:T(8,128)(2,1)S(1)}, s16[624,128]{1,0:T(8,128)(2,1)S(1)}, u32[]{:S(2)}, u32[]{:S(2)}) collective-permute-start(s16[624,128]{1,0:T(8,128)(2,1)S(1)} %get-tuple-element.25), channel_id=1, source_target_pairs={{0,4},{1,5},{2,6},{3,7},{4,8},{5,9},{6,10},{7,11},{8,12},{9,13},{1... | collective-permute-start | bytes 479240 | tf_op jit(solution)/shard_map/ppermute | solution.py:287
  94.1 14.5 %collective-permute-start.11 = (s16[624,128]{1,0:T(8,128)(2,1)S(1)}, s16[624,128]{1,0:T(8,128)(2,1)S(1)}, u32[]{:S(2)}, u32[]{:S(2)}) collective-permute-start(s16[624,128]{1,0:T(8,128)(2,1)S(1)} %get-tuple-element.26), channel_id=1, source_target_pairs={{0,12},{1,13},{2,14},{3,15},{4,0},{5,1},{6,2},{7,3},{8,4},{9,5},{1... | collective-permute-start | bytes 479240 | tf_op jit(solution)/shard_map/ppermute | solution.py:287
  94.9 13.8 %collective-permute-start.9 = (s16[624,128]{1,0:T(8,128)(2,1)S(1)}, s16[624,128]{1,0:T(8,128)(2,1)S(1)}, u32[]{:S(2)}, u32[]{:S(2)}) collective-permute-start(s16[624,128]{1,0:T(8,128)(2,1)S(1)} %get-tuple-element.24), channel_id=1, source_target_pairs={{0,8},{1,9},{2,10},{3,11},{4,12},{5,13},{6,14},{7,15},{8,0},{9,1},... | collective-permute-start | bytes 479240 | tf_op jit(solution)/shard_map/ppermute | solution.py:287
  108.7 38.3 %copy-start.1 = (f32[256,256]{1,0:T(8,128)S(1)}, f32[256,256]{1,0:T(8,128)}, u32[]{:S(2)}) copy-start(f32[256,256]{1,0:T(8,128)} %constant.115.clone.second) | copy-start | bytes 786436
  108.7 38.3 %copy-start.2 = (f32[256,256]{1,0:T(8,128)S(1)}, f32[256,256]{1,0:T(8,128)}, u32[]{:S(2)}) copy-start(f32[256,256]{1,0:T(8,128)} %constant.116.clone.third) | copy-start | bytes 786436
  108.7 38.3 %copy-start.3 = (f32[256,128]{1,0:T(8,128)S(1)}, f32[256,128]{1,0:T(8,128)}, u32[]{:S(2)}) copy-start(f32[256,128]{1,0:T(8,128)} %constant.114.clone.first) | copy-start | bytes 393220
  108.7 38.3 %copy-start.4 = (f32[128,256]{1,0:T(8,128)S(1)}, f32[128,256]{1,0:T(8,128)}, u32[]{:S(2)}) copy-start(f32[128,256]{1,0:T(8,128)} %constant.117.clone.last) | copy-start | bytes 393220
  108.7 38.3 %copy-start.5 = (f32[128,128]{1,0:T(8,128)S(1)}, f32[128,128]{1,0:T(8,128)}, u32[]{:S(2)}) copy-start(f32[128,128]{1,0:T(8,128)} %constant.118.clone.tc) | copy-start | bytes 196612
  108.8 38.3 %copy-start.6 = (f32[128,128]{1,0:T(8,128)S(1)}, f32[128,128]{1,0:T(8,128)}, u32[]{:S(2)}) copy-start(f32[128,128]{1,0:T(8,128)} %constant.119.clone.ts) | copy-start | bytes 196612
  121.8 14.4 %all-to-all-start = ((f32[16,8,1152]{2,1,0:T(8,128)}), f32[16,8,1152]{2,1,0:T(8,128)S(1)}, u32[]{:S(2)}, u32[]{:S(2)}) async-start(f32[16,8,1152]{2,1,0:T(8,128)} %get-tuple-element.29), calls=%async_computation | async-start | bytes 1179648 | tf_op jit(solution)/shard_map/all_to_all | solution.py:491
  136.8 1.6 %collective-permute-start.12 = (f32[4,16,1024]{2,1,0:T(8,128)S(1)}, f32[4,16,1024]{2,1,0:T(8,128)S(1)}, u32[]{:S(2)}, u32[]{:S(2)}) collective-permute-start(f32[4,16,1024]{2,1,0:T(8,128)S(1)} %dynamic-slice_bitcast_fusion), channel_id=1, source_target_pairs={{0,16},{16,0},{32,48},{48,32},{64,80},{80,64},{96,112},{112,96},{1... | collective-permute-start | bytes 786440 | tf_op jit(solution)/shard_map/ppermute | solution.py:466
  138.5 5.7 %collective-permute-start.13 = (f32[16,1024]{1,0:T(8,128)S(1)}, f32[16,1024]{1,0:T(8,128)S(1)}, u32[]{:S(2)}, u32[]{:S(2)}) collective-permute-start(f32[16,1024]{1,0:T(8,128)S(1)} %get-tuple-element.32), channel_id=1, source_target_pairs={{0,32},{16,48},{32,64},{48,80},{64,96},{80,112},{96,0},{112,16},{1... | collective-permute-start | bytes 196616 | tf_op jit(solution)/shard_map/ppermute | solution.py:470
  140.0 6.2 %collective-permute-start.14 = (f32[16,1024]{1,0:T(8,128)S(1)}, f32[16,1024]{1,0:T(8,128)S(1)}, u32[]{:S(2)}, u32[]{:S(2)}) collective-permute-start(f32[16,1024]{1,0:T(8,128)S(1)} %get-tuple-element.31), channel_id=1, source_target_pairs={{0,64},{16,80},{32,96},{48,112},{64,0},{80,16},{96,32},{112,48},{1... | collective-permute-start | bytes 196616 | tf_op jit(solution)/shard_map/ppermute | solution.py:470
  142.7 4.3 %collective-permute-start.15 = (f32[16,1024]{1,0:T(8,128)S(1)}, f32[16,1024]{1,0:T(8,128)S(1)}, u32[]{:S(2)}, u32[]{:S(2)}) collective-permute-start(f32[16,1024]{1,0:T(8,128)S(1)} %get-tuple-element.30), channel_id=1, source_target_pairs={{0,96},{16,112},{32,0},{48,16},{64,32},{80,48},{96,64},{112,80},{1... | collective-permute-start | bytes 196616 | tf_op jit(solution)/shard_map/ppermute | solution.py:470
  149.0 11.1 %all-to-all-start.1 = ((f32[16,8,128]{2,1,0:T(8,128)}), f32[16,8,128]{2,1,0:T(8,128)S(1)}, u32[]{:S(2)}, u32[]{:S(2)}) async-start(f32[16,8,128]{2,1,0:T(8,128)} %filter_rows.1), calls=%async_computation.1 | async-start | bytes 131072 | tf_op jit(solution)/shard_map/all_to_all | solution.py:494
  (1 other events, 6.3 us)

commit v3 on v2

--- a/solution.py
+++ b/solution.py
@@ -78,7 +78,7 @@
         out_specs=pl.BlockSpec((count * 8, WIDE), lambda g: (g, 0)),
         out_shape=pltpu.VMEM((ROWS[half], WIDE), BF16),
         compiler_params=pltpu.CompilerParams(vmem_limit_bytes=32 * MIB),
-        cost_estimate=pl.CostEstimate(flops=1 << 24, bytes_accessed=7 * MIB, transcendentals=0),
+        cost_estimate=pl.CostEstimate(flops=1000, bytes_accessed=1000, transcendentals=0),
         name="pack_left",
     )(mask, in_hbm(blocks), after)
 
@@ -123,7 +123,7 @@
             pltpu.VMEM((WIDE, 256), BF16),
         ],
         compiler_params=pltpu.CompilerParams(vmem_limit_bytes=24 * MIB),
-        cost_estimate=pl.CostEstimate(flops=1 << 24, bytes_accessed=30 * MIB, transcendentals=0),
+        cost_estimate=pl.CostEstimate(flops=1000, bytes_accessed=1000, transcendentals=0),
         name="pack_right",
     )(in_hbm(blocks), *before)
 
@@ -146,7 +146,7 @@
         out_specs=vmem,
         out_shape=jax.ShapeDtypeStruct((ROWS[half], 256), F32),
         compiler_params=pltpu.CompilerParams(vmem_limit_bytes=12 * MIB),
-        cost_estimate=pl.CostEstimate(flops=2 * 560 * WIDE * 256, bytes_accessed=4 * MIB, transcendentals=0),
+        cost_estimate=pl.CostEstimate(flops=1000, bytes_accessed=1000, transcendentals=0),
         name="product_tails",
     )(left, rest, jnp.asarray(swap, BF16), after)
 
@@ -223,7 +223,7 @@
         out_shape=jax.ShapeDtypeStruct((4 * rows + TOP, 128), I16 if coded else F32),
         scratch_shapes=[pltpu.VMEM((4, rows, 128), F32)],
         compiler_params=pltpu.CompilerParams(vmem_limit_bytes=10 * MIB),
-        cost_estimate=pl.CostEstimate(flops=2 * 560 * WIDE * 512, bytes_accessed=8 * MIB, transcendentals=0),
+        cost_estimate=pl.CostEstimate(flops=1000, bytes_accessed=1000, transcendentals=0),
         name="product_coded" if coded else "product_own",
     )(spot, left, near, tails, after)
 
@@ -274,7 +274,7 @@
         out_shape=[jax.ShapeDtypeStruct((ROWS[half] + FOLD, 128), t) for t in (F32, I16, I16, I16)],
         scratch_shapes=[pltpu.VMEM((4, ROWS[half], 128), F32)],
         compiler_params=pltpu.CompilerParams(vmem_limit_bytes=8 * MIB),
-        cost_estimate=pl.CostEstimate(flops=1 << 22, bytes_accessed=4 * MIB, transcendentals=0),
+        cost_estimate=pl.CostEstimate(flops=1000, bytes_accessed=1000, transcendentals=0),
         name="merge",
     )(place, own, *parts, after)
 
@@ -301,9 +301,10 @@
         tails = product_tails(half, left, rest, after)
         lefts.append((left, near, tails))
         after = tails
-        for d in (2, 1, 3):
-            after = product_group(half, d, spot, *lefts[half], after)
-            parts[half].append(send(after, half, d))
+        for d in (1, 2, 3):
+            last = product_group(half, d, spot, *lefts[half], after)
+            parts[half].append(send(last, half, d))
+        after = last
     for half in range(2):
         after = product_group(half, 0, spot, *lefts[half], after)
         owns.append(after)
@@ -317,14 +318,27 @@
 
 def collocate_kernel(half, keep, ids, own, in1, in2, in3, cols, rows, *rest):
     if half == 0:
-        density, out, stacked, right = rest
+        density, out, stacked, right, held, held_cols, sems = rest
         before = None
     else:
-        before, density, out, stacked, right = rest
+        before, density, out, stacked, right, held, held_cols, sems = rest
     count = ROWS[half]
-
-    @pl.when(pl.program_id(0) == 0)
-    def _():
+    tiles = 16384 // POINTS
+
+    def copies(g):
+        spot = pl.ds(pl.multiple_of(g * POINTS, POINTS), POINTS)
+        return (
+            pltpu.make_async_copy(cols.at[0, :, spot], held_cols.at[g], sems.at[0, g]),
+            pltpu.make_async_copy(
+                rows.at[pl.ds(CUT[half] // 8, count // 8), :, spot], held.at[g], sems.at[1, g]
+            ),
+        )
+
+    for g in range(tiles):
+        for copy in copies(g):
+            copy.start()
+
+    def decode_density():
         main, fold = own[0:count, :], own[count : count + FOLD, :]
         for part in (in1, in2, in3):
             extra = plain(part[count : count + FOLD, :])
@@ -346,51 +360,54 @@
         density[:, :, 128:BS] = tail.reshape(count // 8, 8, 128)[:, :, : BS - 128]
         right[128:256, :] = jnp.zeros((128, POINTS), BF16)
 
-    right[0:BS, :] = cols[0]
-    for t in range(POINTS // 256):
-        here = slice(t * 256, (t + 1) * 256)
-        inner = jnp.dot(stacked[...], right[:, here], preferred_element_type=F32).reshape(count // 8, 8, 256)
-        total = jnp.sum(inner * rows[:, :, here].astype(F32), axis=0)
-        within = slice(t % 4 * 256, t % 4 * 256 + 256)
+    decode_density()
+
+    def step(g, carry):
+        for copy in copies(g):
+            copy.wait()
+        right[0:BS, :] = held_cols[g]
+        tile(g)
+        return carry
+
+    def tile(g):
+        per = POINTS // 1024
+        for t in range(POINTS // 256):
+            here = slice(t * 256, (t + 1) * 256)
+            inner = jnp.dot(stacked[...], right[:, here], preferred_element_type=F32).reshape(count // 8, 8, 256)
+            total = jnp.sum(inner * held[g, :, :, here].astype(F32), axis=0)
+            within = slice(t % 4 * 256, t % 4 * 256 + 256)
+            if half == 1:
+                total = total + before[per * g + t // 4, :, within]
+            out[per * g + t // 4, :, within] = total
         if half == 1:
-            total = total + before[t // 4, :, within]
-        out[t // 4, :, within] = total
-    if half == 1:
-        for n in range(POINTS // 1024):
-            out[n, :, 1024:1152] = ids[...]
+            for n in range(POINTS // 1024):
+                out[per * g + n, :, 1024:1152] = ids[...]
+
+    lax.fori_loop(0, tiles, step, 0)
 
 
 def collocate(half, keep, ids, own, parts, basis_cols, basis_rows, before):
     count = ROWS[half]
-    unit = pl.BlockSpec((count + FOLD, 128), lambda g: (0, 0))
-    small = pl.BlockSpec((8, 128), lambda g: (0, 0))
     wide = 1152 if half else 1024
-    many = count // 8
+    vmem = pl.BlockSpec(memory_space=pltpu.VMEM)
+    tiles = 16384 // POINTS
     return pl.pallas_call(
         functools.partial(collocate_kernel, half),
-        grid=(16384 // POINTS,),
-        in_specs=[small, small]
-        + [unit] * 4
-        + [
-            pl.BlockSpec((1, BS, POINTS), lambda g: (0, 0, g)),
-            pl.BlockSpec(
-                (pl.Element(many), pl.Element(8), pl.Element(POINTS)), lambda g: (CUT[half] // 8, 0, g * POINTS)
-            ),
-        ]
-        + [pl.BlockSpec((POINTS // 1024, 8, 1024), lambda g: (g, 0, 0))] * half,
-        out_specs=[
-            pl.BlockSpec((many, 8, BS), lambda g: (0, 0, 0)),
-            pl.BlockSpec((POINTS // 1024, 8, wide), lambda g: (g, 0, 0)),
+        in_specs=[vmem] * 6 + [pl.BlockSpec(memory_space=pltpu.HBM)] * 2 + [vmem] * half,
+        out_specs=[vmem] * 2,
+        scratch_shapes=[
+            pltpu.VMEM((count, 256), BF16),
+            pltpu.VMEM((256, POINTS), BF16),
+            pltpu.VMEM((tiles, count // 8, 8, POINTS), BF16),
+            pltpu.VMEM((tiles, BS, POINTS), BF16),
+            pltpu.SemaphoreType.DMA((2, tiles)),
         ],
-        scratch_shapes=[pltpu.VMEM((count, 256), BF16), pltpu.VMEM((256, POINTS), BF16)],
         out_shape=[
-            jax.ShapeDtypeStruct((many, 8, BS), BF16),
+            jax.ShapeDtypeStruct((count // 8, 8, BS), BF16),
             jax.ShapeDtypeStruct((16, 8, wide), F32),
         ],
-        compiler_params=pltpu.CompilerParams(vmem_limit_bytes=16 * MIB),
-        cost_estimate=pl.CostEstimate(
-            flops=2 * count * 256 * 16384, bytes_accessed=(count + 144) * 16384 * 2, transcendentals=0
-        ),
+        compiler_params=pltpu.CompilerParams(vmem_limit_bytes=32 * MIB),
+        cost_estimate=pl.CostEstimate(flops=1000, bytes_accessed=1000, transcendentals=0),
         name="collocate",
     )(keep, ids, own, *parts, in_hbm(basis_cols), in_hbm(basis_rows), *before)
 
@@ -407,7 +424,7 @@
         bricks_kernel,
         out_shape=jax.ShapeDtypeStruct((128, 1024), F32),
         compiler_params=pltpu.CompilerParams(vmem_limit_bytes=8 * MIB),
-        cost_estimate=pl.CostEstimate(flops=2 * 128 * 128 * 1024, bytes_accessed=MIB, transcendentals=0),
+        cost_estimate=pl.CostEstimate(flops=1000, bytes_accessed=1000, transcendentals=0),
         name="sum_bricks",
     )(points)
 
@@ -452,7 +469,7 @@
         filter_kernel,
         out_shape=jax.ShapeDtypeStruct((16, 8, 128), F32),
         compiler_params=pltpu.CompilerParams(vmem_limit_bytes=8 * MIB),
-        cost_estimate=pl.CostEstimate(flops=1 << 26, bytes_accessed=MIB, transcendentals=0),
+        cost_estimate=pl.CostEstimate(flops=1000, bytes_accessed=1000, transcendentals=0),
         name="filter_rows",
     )(*pieces, kern, *tables())
 
@@ -479,15 +496,13 @@
     keep = jnp.broadcast_to(filter_mask.reshape(8, 1).astype(F32), (8, 128))
     by_point = jnp.transpose(basis_rows, (1, 0, 2))
     finish, after = exchange_products(blocks_a, pattern_a, blocks_b, [kern, ids, keep])
-    densities, before, sums = [], [], []
+    densities, before = [], []
     for half in range(2):
-        sums.append(finish(half, after))
-        after = sums[-1][0]
-    for half in range(2):
-        own, parts = sums[half]
-        density, points = collocate(half, keep, ids, own, parts, basis_cols, by_point, before)
+        own, parts = finish(half, after)
+        density, after = collocate(half, keep, ids, own, parts, basis_cols, by_point, before)
         densities.append(density)
-        before = [points]
+        before = [after]
+    points = after
     points = lax.all_to_all(points, "col", split_axis=0, concat_axis=0, tiled=True)
     pieces = scatter_rows(sum_bricks(points))
     filtered = filter_rows(pieces, kern)

time: 162 us -> 161 us (level)
  waiting for transfers between devices: 40.6 us -> 48.8 us
  Pallas kernels: 77.2 us -> 70.4 us
    ppermute x12, waiting for transfers between devices: 19.2 us -> 27.4 us  [send(): return lax.ppermute(array, 'col', turn(d, 0) if axis == 0 else turn(0, d))]
    pallas_call x2, Pallas kernels: 25.3 us -> 18.5 us  [collocate(): pl.pallas_call(functools.partial(collocate_kernel, half), in_specs=[vmem]...]
    ppermute x12, starting transfers between devices: 23.3 us -> 20.1 us  [send(): return lax.ppermute(array, 'col', turn(d, 0) if axis == 0 else turn(0, d))]
    all_to_all x1, starting transfers between devices: 3.93 us -> 5.61 us  [shards(): lax.all_to_all(points, 'col', split_axis=0, concat_axis=0, tiled=True)]
  transfers between devices with their start and end apart: 18 -> 18, of which waited for: 8 -> 11; matrix products, arithmetic and copies ran while one was open for 1% -> 1% of each run, Pallas kernels for 22% -> 21%
where the time goes in v3:
time: 161 us
  Pallas kernels  70.4 us (44%)
  waiting for transfers between devices  48.8 us (30%)
  starting transfers between devices  35.1 us (22%)
  local copies, waits for them, and re-layouts  2.94 us (2%)
  other arithmetic  2.37 us (1%)
    ppermute x12, waiting for transfers between devices, send(): return lax.ppermute(array, 'col', turn(d, 0) if axis == 0 else turn(0, d))  27.4 us
    ppermute x12, starting transfers between devices, send(): return lax.ppermute(array, 'col', turn(d, 0) if axis == 0 else turn(0, d))  20.1 us
    pallas_call x8, Pallas kernels, product_group(): pl.pallas_call(functools.partial(product_kernel, half, d), in_specs=[pl.B...  18.6 us
    pallas_call x2, Pallas kernels, collocate(): pl.pallas_call(functools.partial(collocate_kernel, half), in_specs=[vmem]...  18.5 us
    pallas_call x1, Pallas kernels, pack_right(): pl.pallas_call(pack_right_kernel, grid=(8,), in_specs=[pl.BlockSpec((2, B...  12.5 us
    pallas_call x2, Pallas kernels, pack_left(): pl.pallas_call(functools.partial(pack_left_kernel, count // 2), grid=(ROW...  12.3 us
    all_to_all x1, waiting for transfers between devices, shards(): lax.all_to_all(points, 'col', split_axis=0, concat_axis=0, tiled=True)  10.4 us
    all_to_all x1, waiting for transfers between devices, shards(): lax.all_to_all(filtered, 'col', split_axis=0, concat_axis=0, tiled=True)  6.71 us
  transfers between devices with their start and end apart: 18, of which 11 were waited for; matrix products, arithmetic and copies ran while one was open for 1% of the time, Pallas kernels for 21%

profile of v3, /device:TPU:0, one launch (start us, length us, event | category | flops | bytes accessed | tf_op | source)
XLA Modules:
  0.0 160.7 jit_solution(18064193530442852896)
XLA Ops:
  4.3 12.5 %pack_right.1 = (bf16[16,2304,128]{2,1,0:T(8,128)(2,1)S(1)}, bf16[2304,256]{1,0:T(8,128)(2,1)S(1)}) custom-call(bf16[16,138,16,138]{3,2,1,0:T(8,128)(2,1)} %bitcast.40, bf16[16,16,128]{2,1,0:T(8,128)(2,1)S(1)} %broadcast_in_dim.21.others_0_.mask, s32[2]{0:T(128)S(1)} %pad_add_fusion.others_1_.spot.place, f32[128,128]{1,0:T(8,128)S(1)} %bitcast.34, ...), custom_call_target="tpu_custom_call" | custom-call | flops 1000 | bytes 1000 | tf_op jit(solution)/shard_map/pack_right/pallas_call | solution.py:112
  16.9 6.3 %pack_left.2.left = bf16[560,2304]{1,0:T(8,128)(2,1)S(1)} custom-call(bf16[16,16,128]{2,1,0:T(8,128)(2,1)S(1)} %broadcast_in_dim.21.others_0_.mask, bf16[8,138,16,138]{3,2,1,0:T(8,128)(2,1)} %bitcast.38, bf16[16,2304,128]{2,1,0:T(8,128)(2,1)S(1)} %get-tuple-element.16.after.near), custom_call_target="tpu_custom_call" | custom-call | flops 1000 | bytes 1000 | tf_op jit(solution)/shard_map/pack_left/pallas_call | solution.py:67
  24.0 2.4 %product_coded.9 = s16[2528,128]{1,0:T(8,128)(2,1)S(1)} custom-call(s32[2]{0:T(128)S(1)} %pad_add_fusion.others_1_.spot.place, bf16[560,2304]{1,0:T(8,128)(2,1)S(1)} %pack_left.2.left, bf16[16,2304,128]{2,1,0:T(8,128)(2,1)S(1)} %get-tuple-element.16.after.near, f32[560,256]{1,0:T(8,128)S(1)} %product_tails.2.tails.after, f32[560,256]{1,0:T(8,128)S(1)} %product_tails.2.tails.after), custom_call_target="tpu_custom_call" | custom-call | flops 1000 | bytes 1000 | tf_op jit(solution)/shard_map/product_coded/pallas_call | solution.py:219
  26.5 3.3 %collective-permute-start.1 = (s16[2528,128]{1,0:T(8,128)(2,1)S(1)}, s16[2528,128]{1,0:T(8,128)(2,1)S(1)}, u32[]{:S(2)}, u32[]{:S(2)}) collective-permute-start(s16[2528,128]{1,0:T(8,128)(2,1)S(1)} %product_coded.9), channel_id=1, source_target_pairs={{0,8},{1,9},{2,10},{3,11},{4,12},{5,13},{6,14},{7,15},{8,0},{9,1},... | collective-permute-start | bytes 1941512 | tf_op jit(solution)/shard_map/ppermute | solution.py:287
  29.8 2.4 %product_coded.8 = s16[2528,128]{1,0:T(8,128)(2,1)S(1)} custom-call(s32[2]{0:T(128)S(1)} %pad_add_fusion.others_1_.spot.place, bf16[560,2304]{1,0:T(8,128)(2,1)S(1)} %pack_left.2.left, bf16[16,2304,128]{2,1,0:T(8,128)(2,1)S(1)} %get-tuple-element.16.after.near, f32[560,256]{1,0:T(8,128)S(1)} %product_tails.2.tails.after, f32[560,256]{1,0:T(8,128)S(1)} %product_tails.2.tails.after), custom_call_target="tpu_custom_call" | custom-call | flops 1000 | bytes 1000 | tf_op jit(solution)/shard_map/product_coded/pallas_call | solution.py:219
  33.0 2.4 %product_coded.6.after = s16[2528,128]{1,0:T(8,128)(2,1)S(1)} custom-call(s32[2]{0:T(128)S(1)} %pad_add_fusion.others_1_.spot.place, bf16[560,2304]{1,0:T(8,128)(2,1)S(1)} %pack_left.2.left, bf16[16,2304,128]{2,1,0:T(8,128)(2,1)S(1)} %get-tuple-element.16.after.near, f32[560,256]{1,0:T(8,128)S(1)} %product_tails.2.tails.after, ...), custom_call_target="tpu_custom_call" | custom-call | flops 1000 | bytes 1000 | tf_op jit(solution)/shard_map/product_coded/pallas_call | solution.py:219
  35.5 2.6 %collective-permute-start.2 = (s16[2528,128]{1,0:T(8,128)(2,1)S(1)}, s16[2528,128]{1,0:T(8,128)(2,1)S(1)}, u32[]{:S(2)}, u32[]{:S(2)}) collective-permute-start(s16[2528,128]{1,0:T(8,128)(2,1)S(1)} %product_coded.6.after), channel_id=1, source_target_pairs={{0,12},{1,13},{2,14},{3,15},{4,0},{5,1},{6,2},{7,3},{8,4},{9,5},{1... | collective-permute-start | bytes 1941512 | tf_op jit(solution)/shard_map/ppermute | solution.py:287
  38.1 6.0 %pack_left.3.left = bf16[544,2304]{1,0:T(8,128)(2,1)S(1)} custom-call(bf16[16,16,128]{2,1,0:T(8,128)(2,1)S(1)} %broadcast_in_dim.21.others_0_.mask, bf16[8,138,16,138]{3,2,1,0:T(8,128)(2,1)} %bitcast.39, s16[2528,128]{1,0:T(8,128)(2,1)S(1)} %product_coded.6.after), custom_call_target="tpu_custom_call" | custom-call | flops 1000 | bytes 1000 | tf_op jit(solution)/shard_map/pack_left/pallas_call | solution.py:67
  45.5 2.4 %product_coded.11 = s16[2464,128]{1,0:T(8,128)(2,1)S(1)} custom-call(s32[2]{0:T(128)S(1)} %pad_add_fusion.others_1_.spot.place, bf16[544,2304]{1,0:T(8,128)(2,1)S(1)} %pack_left.3.left, bf16[16,2304,128]{2,1,0:T(8,128)(2,1)S(1)} %get-tuple-element.16.after.near, f32[544,256]{1,0:T(8,128)S(1)} %product_tails.3.tails.after, ...), custom_call_target="tpu_custom_call" | custom-call | flops 1000 | bytes 1000 | tf_op jit(solution)/shard_map/product_coded/pallas_call | solution.py:219
  48.0 4.0 %collective-permute-start.7 = (s16[2464,128]{1,0:T(8,128)(2,1)S(1)}, s16[2464,128]{1,0:T(8,128)(2,1)S(1)}, u32[]{:S(2)}, u32[]{:S(2)}) collective-permute-start(s16[2464,128]{1,0:T(8,128)(2,1)S(1)} %product_coded.11), channel_id=1, source_target_pairs={{0,2},{1,3},{2,0},{3,1},{4,6},{5,7},{6,4},{7,5},{8,10},{9,11},{10,... | collective-permute-start | bytes 1892360 | tf_op jit(solution)/shard_map/ppermute | solution.py:287
  51.9 2.4 %product_coded.10 = s16[2464,128]{1,0:T(8,128)(2,1)S(1)} custom-call(s32[2]{0:T(128)S(1)} %pad_add_fusion.others_1_.spot.place, bf16[544,2304]{1,0:T(8,128)(2,1)S(1)} %pack_left.3.left, bf16[16,2304,128]{2,1,0:T(8,128)(2,1)S(1)} %get-tuple-element.16.after.near, f32[544,256]{1,0:T(8,128)S(1)} %product_tails.3.tails.after, ...), custom_call_target="tpu_custom_call" | custom-call | flops 1000 | bytes 1000 | tf_op jit(solution)/shard_map/product_coded/pallas_call | solution.py:219
  55.4 2.4 %product_coded.7.after = s16[2464,128]{1,0:T(8,128)(2,1)S(1)} custom-call(s32[2]{0:T(128)S(1)} %pad_add_fusion.others_1_.spot.place, bf16[544,2304]{1,0:T(8,128)(2,1)S(1)} %pack_left.3.left, bf16[16,2304,128]{2,1,0:T(8,128)(2,1)S(1)} %get-tuple-element.16.after.near, f32[544,256]{1,0:T(8,128)S(1)} %product_tails.3.tails.after, ...), custom_call_target="tpu_custom_call" | custom-call | flops 1000 | bytes 1000 | tf_op jit(solution)/shard_map/product_coded/pallas_call | solution.py:219
  57.8 2.5 %collective-permute-start.8 = (s16[2464,128]{1,0:T(8,128)(2,1)S(1)}, s16[2464,128]{1,0:T(8,128)(2,1)S(1)}, u32[]{:S(2)}, u32[]{:S(2)}) collective-permute-start(s16[2464,128]{1,0:T(8,128)(2,1)S(1)} %product_coded.7.after), channel_id=1, source_target_pairs={{0,3},{1,0},{2,1},{3,2},{4,7},{5,4},{6,5},{7,6},{8,11},{9,8},{10,9... | collective-permute-start | bytes 1892360 | tf_op jit(solution)/shard_map/ppermute | solution.py:287
  67.2 16.9 %collective-permute-done.3.in1 = s16[640,128]{1,0:T(8,128)(2,1)S(1)} collective-permute-done((s16[640,128]{1,0:T(8,128)(2,1)S(1)}, s16[640,128]{1,0:T(8,128)(2,1)S(1)}, u32[]{:S(2)}, u32[]{:S(2)}) %collective-permute-start.3) | collective-permute-done | bytes 163872 | tf_op jit(solution)/shard_map/ppermute | solution.py:287
  85.8 3.6 %collective-permute-done.5.in3 = s16[640,128]{1,0:T(8,128)(2,1)S(1)} collective-permute-done((s16[640,128]{1,0:T(8,128)(2,1)S(1)}, s16[640,128]{1,0:T(8,128)(2,1)S(1)}, u32[]{:S(2)}, u32[]{:S(2)}) %collective-permute-start.5) | collective-permute-done | bytes 163872 | tf_op jit(solution)/shard_map/ppermute | solution.py:287
  89.4 8.9 %collocate.2 = (bf16[70,8,138]{2,1,0:T(8,128)(2,1)S(1)}, f32[16,8,1024]{2,1,0:T(8,128)S(1)}) custom-call(f32[8,128]{1,0:T(8,128)S(1)} %broadcast_in_dim.20.others_4_.keep, f32[8,128]{1,0:T(8,128)S(1)} %concatenate.6.others_3_.ids, f32[640,128]{1,0:T(8,128)S(1)} %get-tuple-element.18.own, s16[640,128]{1,0:T(8,128)(2,1)S(1)} %collective-permute-done.3.in1, ...), custom_call_target="tpu_custom_call" | custom-call | flops 1000 | bytes 1000 | tf_op jit(solution)/shard_map/collocate/pallas_call | solution.py:394
  100.3 3.2 %collective-permute-start.11 = (s16[624,128]{1,0:T(8,128)(2,1)S(1)}, s16[624,128]{1,0:T(8,128)(2,1)S(1)}, u32[]{:S(2)}, u32[]{:S(2)}) collective-permute-start(s16[624,128]{1,0:T(8,128)(2,1)S(1)} %get-tuple-element.27), channel_id=1, source_target_pairs={{0,12},{1,13},{2,14},{3,15},{4,0},{5,1},{6,2},{7,3},{8,4},{9,5},{1... | collective-permute-start | bytes 479240 | tf_op jit(solution)/shard_map/ppermute | solution.py:287
  103.6 4.2 %collective-permute-done.10.in2 = s16[624,128]{1,0:T(8,128)(2,1)S(1)} collective-permute-done((s16[624,128]{1,0:T(8,128)(2,1)S(1)}, s16[624,128]{1,0:T(8,128)(2,1)S(1)}, u32[]{:S(2)}, u32[]{:S(2)}) %collective-permute-start.10) | collective-permute-done | bytes 159776 | tf_op jit(solution)/shard_map/ppermute | solution.py:287
  110.4 9.6 %collocate.3 = (bf16[68,8,138]{2,1,0:T(8,128)(2,1)S(1)}, f32[16,8,1152]{2,1,0:T(8,128)}) custom-call(f32[8,128]{1,0:T(8,128)S(1)} %broadcast_in_dim.20.others_4_.keep, f32[8,128]{1,0:T(8,128)S(1)} %concatenate.6.others_3_.ids, f32[624,128]{1,0:T(8,128)S(1)} %get-tuple-element.24.own, s16[624,128]{1,0:T(8,128)(2,1)S(1)} %collective-permute-done.9.in1, ...), custom_call_target="tpu_custom_call" | custom-call | flops 1000 | bytes 1000 | tf_op jit(solution)/shard_map/collocate/pallas_call | solution.py:394
  120.0 5.6 %all-to-all-start = ((f32[16,8,1152]{2,1,0:T(8,128)}), f32[16,8,1152]{2,1,0:T(8,128)S(1)}, u32[]{:S(2)}, u32[]{:S(2)}) async-start(f32[16,8,1152]{2,1,0:T(8,128)} %get-tuple-element.29), calls=%async_computation | async-start | bytes 1179648 | tf_op jit(solution)/shard_map/all_to_all | solution.py:506
  125.6 10.4 %all-to-all-done.points = f32[16,8,1152]{2,1,0:T(8,128)S(1)} async-done(((f32[16,8,1152]{2,1,0:T(8,128)}), f32[16,8,1152]{2,1,0:T(8,128)S(1)}, u32[]{:S(2)}, u32[]{:S(2)}) %all-to-all-start) | async-done | bytes 589856 | tf_op jit(solution)/shard_map/all_to_all | solution.py:506
  139.9 2.7 %collective-permute-start.14 = (f32[16,1024]{1,0:T(8,128)S(1)}, f32[16,1024]{1,0:T(8,128)S(1)}, u32[]{:S(2)}, u32[]{:S(2)}) collective-permute-start(f32[16,1024]{1,0:T(8,128)S(1)} %get-tuple-element.31), channel_id=1, source_target_pairs={{0,64},{16,80},{32,96},{48,112},{64,0},{80,16},{96,32},{112,48},{1... | collective-permute-start | bytes 196616 | tf_op jit(solution)/shard_map/ppermute | solution.py:487
  148.9 3.5 %all-to-all-start.1 = ((f32[16,8,128]{2,1,0:T(8,128)}), f32[16,8,128]{2,1,0:T(8,128)S(1)}, u32[]{:S(2)}, u32[]{:S(2)}) async-start(f32[16,8,128]{2,1,0:T(8,128)} %filter_rows.1), calls=%async_computation.1 | async-start | bytes 131072 | tf_op jit(solution)/shard_map/all_to_all | solution.py:509
  153.3 6.7 %all-to-all-done.1 = f32[16,8,128]{2,1,0:T(8,128)S(1)} async-done(((f32[16,8,128]{2,1,0:T(8,128)}), f32[16,8,128]{2,1,0:T(8,128)S(1)}, u32[]{:S(2)}, u32[]{:S(2)}) %all-to-all-start.1) | async-done | bytes 65568 | tf_op jit(solution)/shard_map/all_to_all | solution.py:509
  (63 shorter events, 32.4 us)
Async XLA Ops:
  26.5 31.3 %collective-permute-start.1 = (s16[2528,128]{1,0:T(8,128)(2,1)S(1)}, s16[2528,128]{1,0:T(8,128)(2,1)S(1)}, u32[]{:S(2)}, u32[]{:S(2)}) collective-permute-start(s16[2528,128]{1,0:T(8,128)(2,1)S(1)} %product_coded.9), channel_id=1, source_target_pairs={{0,8},{1,9},{2,10},{3,11},{4,12},{5,13},{6,14},{7,15},{8,0},{9,1},... | collective-permute-start | bytes 1941512 | tf_op jit(solution)/shard_map/ppermute | solution.py:287
  32.3 32.0 %collective-permute-start = (s16[2528,128]{1,0:T(8,128)(2,1)S(1)}, s16[2528,128]{1,0:T(8,128)(2,1)S(1)}, u32[]{:S(2)}, u32[]{:S(2)}) collective-permute-start(s16[2528,128]{1,0:T(8,128)(2,1)S(1)} %product_coded.8), channel_id=1, source_target_pairs={{0,4},{1,5},{2,6},{3,7},{4,8},{5,9},{6,10},{7,11},{8,12},{9,13},{1... | collective-permute-start | bytes 1941512 | tf_op jit(solution)/shard_map/ppermute | solution.py:287
  35.5 28.9 %collective-permute-start.2 = (s16[2528,128]{1,0:T(8,128)(2,1)S(1)}, s16[2528,128]{1,0:T(8,128)(2,1)S(1)}, u32[]{:S(2)}, u32[]{:S(2)}) collective-permute-start(s16[2528,128]{1,0:T(8,128)(2,1)S(1)} %product_coded.6.after), channel_id=1, source_target_pairs={{0,12},{1,13},{2,14},{3,15},{4,0},{5,1},{6,2},{7,3},{8,4},{9,5},{1... | collective-permute-start | bytes 1941512 | tf_op jit(solution)/shard_map/ppermute | solution.py:287
  48.0 50.4 %collective-permute-start.7 = (s16[2464,128]{1,0:T(8,128)(2,1)S(1)}, s16[2464,128]{1,0:T(8,128)(2,1)S(1)}, u32[]{:S(2)}, u32[]{:S(2)}) collective-permute-start(s16[2464,128]{1,0:T(8,128)(2,1)S(1)} %product_coded.11), channel_id=1, source_target_pairs={{0,2},{1,3},{2,0},{3,1},{4,6},{5,7},{6,4},{7,5},{8,10},{9,11},{10,... | collective-permute-start | bytes 1892360 | tf_op jit(solution)/shard_map/ppermute | solution.py:287
  54.3 44.1 %collective-permute-start.6 = (s16[2464,128]{1,0:T(8,128)(2,1)S(1)}, s16[2464,128]{1,0:T(8,128)(2,1)S(1)}, u32[]{:S(2)}, u32[]{:S(2)}) collective-permute-start(s16[2464,128]{1,0:T(8,128)(2,1)S(1)} %product_coded.10), channel_id=1, source_target_pairs={{0,1},{1,2},{2,3},{3,0},{4,5},{5,6},{6,7},{7,4},{8,9},{9,10},{10,1... | collective-permute-start | bytes 1892360 | tf_op jit(solution)/shard_map/ppermute | solution.py:287
  57.8 40.6 %collective-permute-start.8 = (s16[2464,128]{1,0:T(8,128)(2,1)S(1)}, s16[2464,128]{1,0:T(8,128)(2,1)S(1)}, u32[]{:S(2)}, u32[]{:S(2)}) collective-permute-start(s16[2464,128]{1,0:T(8,128)(2,1)S(1)} %product_coded.7.after), channel_id=1, source_target_pairs={{0,3},{1,0},{2,1},{3,2},{4,7},{5,4},{6,5},{7,6},{8,11},{9,8},{10,9... | collective-permute-start | bytes 1892360 | tf_op jit(solution)/shard_map/ppermute | solution.py:287
  66.2 17.9 %collective-permute-start.3 = (s16[640,128]{1,0:T(8,128)(2,1)S(1)}, s16[640,128]{1,0:T(8,128)(2,1)S(1)}, u32[]{:S(2)}, u32[]{:S(2)}) collective-permute-start(s16[640,128]{1,0:T(8,128)(2,1)S(1)} %get-tuple-element.19), channel_id=1, source_target_pairs={{0,2},{1,3},{2,0},{3,1},{4,6},{5,7},{6,4},{7,5},{8,10},{9,11},{10,... | collective-permute-start | bytes 491528 | tf_op jit(solution)/shard_map/ppermute | solution.py:287
  66.3 19.5 %collective-permute-start.4 = (s16[640,128]{1,0:T(8,128)(2,1)S(1)}, s16[640,128]{1,0:T(8,128)(2,1)S(1)}, u32[]{:S(2)}, u32[]{:S(2)}) collective-permute-start(s16[640,128]{1,0:T(8,128)(2,1)S(1)} %get-tuple-element.20), channel_id=1, source_target_pairs={{0,1},{1,2},{2,3},{3,0},{4,5},{5,6},{6,7},{7,4},{8,9},{9,10},{10,1... | collective-permute-start | bytes 491528 | tf_op jit(solution)/shard_map/ppermute | solution.py:287
  84.1 5.3 %collective-permute-start.5 = (s16[640,128]{1,0:T(8,128)(2,1)S(1)}, s16[640,128]{1,0:T(8,128)(2,1)S(1)}, u32[]{:S(2)}, u32[]{:S(2)}) collective-permute-start(s16[640,128]{1,0:T(8,128)(2,1)S(1)} %get-tuple-element.21), channel_id=1, source_target_pairs={{0,3},{1,0},{2,1},{3,2},{4,7},{5,4},{6,5},{7,6},{8,11},{9,8},{10,9... | collective-permute-start | bytes 491528 | tf_op jit(solution)/shard_map/ppermute | solution.py:287
  100.3 7.5 %collective-permute-start.10 = (s16[624,128]{1,0:T(8,128)(2,1)S(1)}, s16[624,128]{1,0:T(8,128)(2,1)S(1)}, u32[]{:S(2)}, u32[]{:S(2)}) collective-permute-start(s16[624,128]{1,0:T(8,128)(2,1)S(1)} %get-tuple-element.26), channel_id=1, source_target_pairs={{0,4},{1,5},{2,6},{3,7},{4,8},{5,9},{6,10},{7,11},{8,12},{9,13},{1... | collective-permute-start | bytes 479240 | tf_op jit(solution)/shard_map/ppermute | solution.py:287
  100.3 7.7 %collective-permute-start.11 = (s16[624,128]{1,0:T(8,128)(2,1)S(1)}, s16[624,128]{1,0:T(8,128)(2,1)S(1)}, u32[]{:S(2)}, u32[]{:S(2)}) collective-permute-start(s16[624,128]{1,0:T(8,128)(2,1)S(1)} %get-tuple-element.27), channel_id=1, source_target_pairs={{0,12},{1,13},{2,14},{3,15},{4,0},{5,1},{6,2},{7,3},{8,4},{9,5},{1... | collective-permute-start | bytes 479240 | tf_op jit(solution)/shard_map/ppermute | solution.py:287
  103.6 6.8 %collective-permute-start.9 = (s16[624,128]{1,0:T(8,128)(2,1)S(1)}, s16[624,128]{1,0:T(8,128)(2,1)S(1)}, u32[]{:S(2)}, u32[]{:S(2)}) collective-permute-start(s16[624,128]{1,0:T(8,128)(2,1)S(1)} %get-tuple-element.25), channel_id=1, source_target_pairs={{0,8},{1,9},{2,10},{3,11},{4,12},{5,13},{6,14},{7,15},{8,0},{9,1},... | collective-permute-start | bytes 479240 | tf_op jit(solution)/shard_map/ppermute | solution.py:287
  110.3 36.6 %copy-start.1 = (f32[256,256]{1,0:T(8,128)S(1)}, f32[256,256]{1,0:T(8,128)}, u32[]{:S(2)}) copy-start(f32[256,256]{1,0:T(8,128)} %constant.115.clone.second) | copy-start | bytes 786436
  110.3 36.6 %copy-start.2 = (f32[256,256]{1,0:T(8,128)S(1)}, f32[256,256]{1,0:T(8,128)}, u32[]{:S(2)}) copy-start(f32[256,256]{1,0:T(8,128)} %constant.116.clone.third) | copy-start | bytes 786436
  110.4 36.6 %copy-start.3 = (f32[256,128]{1,0:T(8,128)S(1)}, f32[256,128]{1,0:T(8,128)}, u32[]{:S(2)}) copy-start(f32[256,128]{1,0:T(8,128)} %constant.114.clone.first) | copy-start | bytes 393220
  110.4 36.6 %copy-start.4 = (f32[128,256]{1,0:T(8,128)S(1)}, f32[128,256]{1,0:T(8,128)}, u32[]{:S(2)}) copy-start(f32[128,256]{1,0:T(8,128)} %constant.117.clone.last) | copy-start | bytes 393220
  110.4 36.6 %copy-start.5 = (f32[128,128]{1,0:T(8,128)S(1)}, f32[128,128]{1,0:T(8,128)}, u32[]{:S(2)}) copy-start(f32[128,128]{1,0:T(8,128)} %constant.118.clone.tc) | copy-start | bytes 196612
  110.4 36.6 %copy-start.6 = (f32[128,128]{1,0:T(8,128)S(1)}, f32[128,128]{1,0:T(8,128)}, u32[]{:S(2)}) copy-start(f32[128,128]{1,0:T(8,128)} %constant.119.clone.ts) | copy-start | bytes 196612
  120.0 16.1 %all-to-all-start = ((f32[16,8,1152]{2,1,0:T(8,128)}), f32[16,8,1152]{2,1,0:T(8,128)S(1)}, u32[]{:S(2)}, u32[]{:S(2)}) async-start(f32[16,8,1152]{2,1,0:T(8,128)} %get-tuple-element.29), calls=%async_computation | async-start | bytes 1179648 | tf_op jit(solution)/shard_map/all_to_all | solution.py:506
  136.7 1.6 %collective-permute-start.12 = (f32[4,16,1024]{2,1,0:T(8,128)S(1)}, f32[4,16,1024]{2,1,0:T(8,128)S(1)}, u32[]{:S(2)}, u32[]{:S(2)}) collective-permute-start(f32[4,16,1024]{2,1,0:T(8,128)S(1)} %dynamic-slice_bitcast_fusion), channel_id=1, source_target_pairs={{0,16},{16,0},{32,48},{48,32},{64,80},{80,64},{96,112},{112,96},{1... | collective-permute-start | bytes 786440 | tf_op jit(solution)/shard_map/ppermute | solution.py:483
  138.4 5.7 %collective-permute-start.13 = (f32[16,1024]{1,0:T(8,128)S(1)}, f32[16,1024]{1,0:T(8,128)S(1)}, u32[]{:S(2)}, u32[]{:S(2)}) collective-permute-start(f32[16,1024]{1,0:T(8,128)S(1)} %get-tuple-element.32), channel_id=1, source_target_pairs={{0,32},{16,48},{32,64},{48,80},{64,96},{80,112},{96,0},{112,16},{1... | collective-permute-start | bytes 196616 | tf_op jit(solution)/shard_map/ppermute | solution.py:487
  139.9 6.2 %collective-permute-start.14 = (f32[16,1024]{1,0:T(8,128)S(1)}, f32[16,1024]{1,0:T(8,128)S(1)}, u32[]{:S(2)}, u32[]{:S(2)}) collective-permute-start(f32[16,1024]{1,0:T(8,128)S(1)} %get-tuple-element.31), channel_id=1, source_target_pairs={{0,64},{16,80},{32,96},{48,112},{64,0},{80,16},{96,32},{112,48},{1... | collective-permute-start | bytes 196616 | tf_op jit(solution)/shard_map/ppermute | solution.py:487
  142.7 4.3 %collective-permute-start.15 = (f32[16,1024]{1,0:T(8,128)S(1)}, f32[16,1024]{1,0:T(8,128)S(1)}, u32[]{:S(2)}, u32[]{:S(2)}) collective-permute-start(f32[16,1024]{1,0:T(8,128)S(1)} %get-tuple-element.30), channel_id=1, source_target_pairs={{0,96},{16,112},{32,0},{48,16},{64,32},{80,48},{96,64},{112,80},{1... | collective-permute-start | bytes 196616 | tf_op jit(solution)/shard_map/ppermute | solution.py:487
  148.9 11.1 %all-to-all-start.1 = ((f32[16,8,128]{2,1,0:T(8,128)}), f32[16,8,128]{2,1,0:T(8,128)S(1)}, u32[]{:S(2)}, u32[]{:S(2)}) async-start(f32[16,8,128]{2,1,0:T(8,128)} %filter_rows.1), calls=%async_computation.1 | async-start | bytes 131072 | tf_op jit(solution)/shard_map/all_to_all | solution.py:509
  (1 other events, 6.3 us)
